TPU v7x, 512 devices: a whole 4x8x8 slice. The times are simulated.
512 devices in a mesh: blk: 32 (over y, z_hi, core), grp: 16 (over x, z_lo).
Axes of the slice: x: 4, y: 8, z: 8 (z_hi: 2, z_lo: 4; z = z_hi * 4 + z_lo), core: 2. Of those that a mesh axis runs over, the one named last changes fastest.
Arguments:
- images: bfloat16 [262144, 1152], P(('blk', 'grp')), may hold values from -0.17675781 to 0.17675781
- texts: bfloat16 [512, 1152], P(('blk', 'grp')), may hold values from -0.17675781 to 0.17675781
- labels: int32 [262144], P(('blk', 'grp')), may hold values from 0 to 511
- log_scale: float32 [1], replicated, may hold values from 3.9 to 4.6
- bias: float32 [1], replicated, may hold values from -6 to -2
- loss_scale: float32 [1], replicated, may hold values from 8192 to 32768
Outputs:
- grad_image: bfloat16 [262144, 1152], P(('blk', 'grp'))
- grad_text: bfloat16 [512, 1152], P(('blk', 'grp'))
Inputs may be any that keep to these rules, and one draw needn't show every extreme that they name: labels[i] is the caption paired with frame i; a caption has many frames.
All inputs are finite; a program needn't handle non-finite values.
Results may differ from a plain program's by a relative error of at most 0.0047.
Values may be sent and summed in bfloat16 or wider, within the bound.
No kernel may reach another device: no remote copies, remote signals or barrier semaphores. Data moves between devices by JAX's collectives and lax.ppermute only.
A program may use at most 64 MiB of HBM per device.

v0:
```python
import jax
import jax.numpy as jnp
from jax import lax
from jax.sharding import PartitionSpec as P


def from_behind(array, axis, by):
    peers = lax.axis_size(axis)
    return lax.ppermute(array, axis, [(i, (i + by) % peers) for i in range(peers)])


def tile_terms(images, labels, text_block, columns, factor, offset, weight):
    logits = (
        factor
        * lax.dot_general(
            images, text_block, (((1,), (1,)), ((), ())), preferred_element_type=jnp.float32
        )
        + offset
    )
    pair_sign = jnp.where(labels[:, None] == columns[None, :], 1.0, -1.0).astype(jnp.float32)
    coefficient = (-pair_sign * jax.nn.sigmoid(-pair_sign * logits) * weight).astype(jnp.bfloat16)
    text_part = lax.dot_general(
        coefficient, images, (((0,), (0,)), ((), ())), preferred_element_type=jnp.float32
    )
    return (coefficient, text_part)


def local(images, texts, labels, log_scale, bias, loss_scale):
    loop_size = lax.axis_size("blk")
    group_size = lax.axis_size("grp")
    position = lax.axis_index("blk")
    factor = jnp.exp(log_scale[0])
    offset = bias[0]
    weight = factor * loss_scale[0] / (images.shape[0] * loop_size * group_size)
    width = texts.shape[1]
    rows_here = images.shape[0]
    group_block = lax.all_gather(texts, "grp", axis=0, tiled=True)
    span = group_block.shape[0]
    total = span * loop_size

    def advance_one(step_index, state_tuple):
        text_block, riding_grad, text_store, coef_store = state_tuple
        block_start = (position - step_index) % loop_size * span
        columns = block_start + jnp.arange(span, dtype=jnp.int32)
        coefficient, text_part = tile_terms(
            images, labels, text_block, columns, factor, offset, weight
        )
        text_store = lax.dynamic_update_slice_in_dim(text_store, text_block, block_start, 0)
        coef_store = lax.dynamic_update_slice_in_dim(coef_store, coefficient, block_start, 1)
        riding_grad = riding_grad + text_part
        text_block = from_behind(text_block, "blk", 1)
        riding_grad = from_behind(riding_grad, "blk", 1)
        return (text_block, riding_grad, text_store, coef_store)

    start_state = (
        group_block,
        jnp.zeros((span, width), jnp.float32),
        jnp.zeros((total, width), jnp.bfloat16),
        jnp.zeros((rows_here, total), jnp.bfloat16),
    )
    final_state = lax.fori_loop(0, loop_size, advance_one, start_state)
    image_grad = jnp.dot(final_state[3], final_state[2], preferred_element_type=jnp.float32)
    text_grad = lax.psum_scatter(final_state[1], "grp", scatter_dimension=0, tiled=True)
    return (image_grad.astype(jnp.bfloat16), text_grad.astype(jnp.bfloat16))


def solution(mesh):
    placed = (P(("blk", "grp"), None), P(("blk", "grp"), None), P(("blk", "grp")), P(), P(), P())
    return jax.shard_map(
        local,
        mesh=mesh,
        in_specs=placed,
        out_specs=(P(("blk", "grp"), None), P(("blk", "grp"), None)),
        check_vma=False,
    )
```

profile of v0, /device:TPU:6, one launch (start us, length us, event | category | flops | bytes accessed | tf_op | source)
XLA Modules:
  0.0 602.2 jit_solution(7608305531741105932)
XLA Ops:
  2.1 38.9 %all-gather = bf16[16,1,1152]{2,1,0:T(2,128)(2,1)S(1)} all-gather(bf16[1,1,1152]{2,1,0:T(2,128)(2,1)} %bitcast.24), channel_id=1, replica_groups=mesh['blk'=32,'grp'=16] {'grp'}, dimensions={0}, use_global_device_ids=true | all-gather | bytes 39168 | tf_op jit(solution)/shard_map/all_gather | solution.py:37
  41.2 484.5 %while.21 = (s32[]{:T(128)}, bf16[16,1152]{1,0:T(8,128)(2,1)S(1)}, f32[16,1152]{1,0:T(8,128)S(1)}, bf16[512,1152]{1,0:T(8,128)(2,1)S(1)}, bf16[512,512]{0,1:T(8,...) while((s32[]{:T(128)}, bf16[16,1152]{1,0:T(8,128)(2,1)S(1)}, ...), condition=%wide.region_1.2_spmd, body=%wide.region_0.1_spmd.sunk | while | flops 37865504 | bytes 3185644 | solution.py:61
  44.6 8.3 %collective-permute-start.1 = (f32[16,1152]{1,0:T(8,128)S(1)}, f32[16,1152]{1,0:T(8,128)S(1)}, u32[]{:S(2)}, u32[]{:S(2)}) collective-permute-start(f32[16,1152]{1,0:T(8,128)S(1)} %convolution_add_fusion.2), channel_id=1, source_target_pairs={{0,16},{16,32},{32,48},{48,64},{64,80},{80,96},{96,112},{112,128},... | collective-permute-start | bytes 221192 | tf_op jit(solution)/shard_map/while/body/eval_jaxpr/ppermute | solution.py:9
  92.8 6.0 collective-permute-done
  107.9 6.0 collective-permute-done
  123.0 6.0 collective-permute-done
  138.1 6.0 collective-permute-done
  153.2 6.0 collective-permute-done
  168.3 6.0 collective-permute-done
  183.4 6.0 collective-permute-done
  198.5 6.0 collective-permute-done
  213.6 6.0 collective-permute-done
  228.7 6.0 collective-permute-done
  243.8 6.0 collective-permute-done
  259.0 6.0 collective-permute-done
  274.1 6.0 collective-permute-done
  289.2 6.0 collective-permute-done
  304.3 6.0 collective-permute-done
  319.4 6.0 collective-permute-done
  334.5 6.0 collective-permute-done
  349.6 6.0 collective-permute-done
  364.7 6.0 collective-permute-done
  379.8 6.0 collective-permute-done
  395.0 6.0 collective-permute-done
  410.1 6.0 collective-permute-done
  425.2 6.0 collective-permute-done
  440.3 6.0 collective-permute-done
  455.4 6.0 collective-permute-done
  470.5 6.0 collective-permute-done
  485.6 6.0 collective-permute-done
  500.7 6.0 collective-permute-done
  527.6 72.0 %all-reduce = bf16[16,1152]{1,0:T(8,128)(2,1)S(1)} all-reduce(f32[16,1152]{1,0:T(8,128)S(1)} %get-tuple-element.271), channel_id=2, replica_groups=mesh['blk'=32,'grp'=16] {'grp'}, use_global_device_ids=true, to_apply=%region_2.3.clone | all-reduce | flops 18432 | bytes 110592
  (270 shorter events, 310.1 us)
Async XLA Ops:
  44.6 12.2 %collective-permute-start.1 = (f32[16,1152]{1,0:T(8,128)S(1)}, f32[16,1152]{1,0:T(8,128)S(1)}, u32[]{:S(2)}, u32[]{:S(2)}) collective-permute-start(f32[16,1152]{1,0:T(8,128)S(1)} %convolution_add_fusion.2), channel_id=1, source_target_pairs={{0,16},{16,32},{32,48},{48,64},{64,80},{80,96},{96,112},{112,128},... | collective-permute-start | bytes 221192 | tf_op jit(solution)/shard_map/while/body/eval_jaxpr/ppermute | solution.py:9
  60.0 12.4 %collective-permute-start.1 = (f32[16,1152]{1,0:T(8,128)S(1)}, f32[16,1152]{1,0:T(8,128)S(1)}, u32[]{:S(2)}, u32[]{:S(2)}) collective-permute-start(f32[16,1152]{1,0:T(8,128)S(1)} %convolution_add_fusion.2), channel_id=1, source_target_pairs={{0,16},{16,32},{32,48},{48,64},{64,80},{80,96},{96,112},{112,128},... | collective-permute-start | bytes 221192 | tf_op jit(solution)/shard_map/while/body/eval_jaxpr/ppermute | solution.py:9
  75.7 11.8 %collective-permute-start.1 = (f32[16,1152]{1,0:T(8,128)S(1)}, f32[16,1152]{1,0:T(8,128)S(1)}, u32[]{:S(2)}, u32[]{:S(2)}) collective-permute-start(f32[16,1152]{1,0:T(8,128)S(1)} %convolution_add_fusion.2), channel_id=1, source_target_pairs={{0,16},{16,32},{32,48},{48,64},{64,80},{80,96},{96,112},{112,128},... | collective-permute-start | bytes 221192 | tf_op jit(solution)/shard_map/while/body/eval_jaxpr/ppermute | solution.py:9
  90.8 11.8 %collective-permute-start.1 = (f32[16,1152]{1,0:T(8,128)S(1)}, f32[16,1152]{1,0:T(8,128)S(1)}, u32[]{:S(2)}, u32[]{:S(2)}) collective-permute-start(f32[16,1152]{1,0:T(8,128)S(1)} %convolution_add_fusion.2), channel_id=1, source_target_pairs={{0,16},{16,32},{32,48},{48,64},{64,80},{80,96},{96,112},{112,128},... | collective-permute-start | bytes 221192 | tf_op jit(solution)/shard_map/while/body/eval_jaxpr/ppermute | solution.py:9
  105.9 11.8 %collective-permute-start.1 = (f32[16,1152]{1,0:T(8,128)S(1)}, f32[16,1152]{1,0:T(8,128)S(1)}, u32[]{:S(2)}, u32[]{:S(2)}) collective-permute-start(f32[16,1152]{1,0:T(8,128)S(1)} %convolution_add_fusion.2), channel_id=1, source_target_pairs={{0,16},{16,32},{32,48},{48,64},{64,80},{80,96},{96,112},{112,128},... | collective-permute-start | bytes 221192 | tf_op jit(solution)/shard_map/while/body/eval_jaxpr/ppermute | solution.py:9
  121.0 11.8 %collective-permute-start.1 = (f32[16,1152]{1,0:T(8,128)S(1)}, f32[16,1152]{1,0:T(8,128)S(1)}, u32[]{:S(2)}, u32[]{:S(2)}) collective-permute-start(f32[16,1152]{1,0:T(8,128)S(1)} %convolution_add_fusion.2), channel_id=1, source_target_pairs={{0,16},{16,32},{32,48},{48,64},{64,80},{80,96},{96,112},{112,128},... | collective-permute-start | bytes 221192 | tf_op jit(solution)/shard_map/while/body/eval_jaxpr/ppermute | solution.py:9
  136.1 11.8 %collective-permute-start.1 = (f32[16,1152]{1,0:T(8,128)S(1)}, f32[16,1152]{1,0:T(8,128)S(1)}, u32[]{:S(2)}, u32[]{:S(2)}) collective-permute-start(f32[16,1152]{1,0:T(8,128)S(1)} %convolution_add_fusion.2), channel_id=1, source_target_pairs={{0,16},{16,32},{32,48},{48,64},{64,80},{80,96},{96,112},{112,128},... | collective-permute-start | bytes 221192 | tf_op jit(solution)/shard_map/while/body/eval_jaxpr/ppermute | solution.py:9
  151.2 11.8 %collective-permute-start.1 = (f32[16,1152]{1,0:T(8,128)S(1)}, f32[16,1152]{1,0:T(8,128)S(1)}, u32[]{:S(2)}, u32[]{:S(2)}) collective-permute-start(f32[16,1152]{1,0:T(8,128)S(1)} %convolution_add_fusion.2), channel_id=1, source_target_pairs={{0,16},{16,32},{32,48},{48,64},{64,80},{80,96},{96,112},{112,128},... | collective-permute-start | bytes 221192 | tf_op jit(solution)/shard_map/while/body/eval_jaxpr/ppermute | solution.py:9
  166.3 11.8 %collective-permute-start.1 = (f32[16,1152]{1,0:T(8,128)S(1)}, f32[16,1152]{1,0:T(8,128)S(1)}, u32[]{:S(2)}, u32[]{:S(2)}) collective-permute-start(f32[16,1152]{1,0:T(8,128)S(1)} %convolution_add_fusion.2), channel_id=1, source_target_pairs={{0,16},{16,32},{32,48},{48,64},{64,80},{80,96},{96,112},{112,128},... | collective-permute-start | bytes 221192 | tf_op jit(solution)/shard_map/while/body/eval_jaxpr/ppermute | solution.py:9
  181.5 11.8 %collective-permute-start.1 = (f32[16,1152]{1,0:T(8,128)S(1)}, f32[16,1152]{1,0:T(8,128)S(1)}, u32[]{:S(2)}, u32[]{:S(2)}) collective-permute-start(f32[16,1152]{1,0:T(8,128)S(1)} %convolution_add_fusion.2), channel_id=1, source_target_pairs={{0,16},{16,32},{32,48},{48,64},{64,80},{80,96},{96,112},{112,128},... | collective-permute-start | bytes 221192 | tf_op jit(solution)/shard_map/while/body/eval_jaxpr/ppermute | solution.py:9
  196.6 11.8 %collective-permute-start.1 = (f32[16,1152]{1,0:T(8,128)S(1)}, f32[16,1152]{1,0:T(8,128)S(1)}, u32[]{:S(2)}, u32[]{:S(2)}) collective-permute-start(f32[16,1152]{1,0:T(8,128)S(1)} %convolution_add_fusion.2), channel_id=1, source_target_pairs={{0,16},{16,32},{32,48},{48,64},{64,80},{80,96},{96,112},{112,128},... | collective-permute-start | bytes 221192 | tf_op jit(solution)/shard_map/while/body/eval_jaxpr/ppermute | solution.py:9
  211.7 11.8 %collective-permute-start.1 = (f32[16,1152]{1,0:T(8,128)S(1)}, f32[16,1152]{1,0:T(8,128)S(1)}, u32[]{:S(2)}, u32[]{:S(2)}) collective-permute-start(f32[16,1152]{1,0:T(8,128)S(1)} %convolution_add_fusion.2), channel_id=1, source_target_pairs={{0,16},{16,32},{32,48},{48,64},{64,80},{80,96},{96,112},{112,128},... | collective-permute-start | bytes 221192 | tf_op jit(solution)/shard_map/while/body/eval_jaxpr/ppermute | solution.py:9
  226.8 11.8 %collective-permute-start.1 = (f32[16,1152]{1,0:T(8,128)S(1)}, f32[16,1152]{1,0:T(8,128)S(1)}, u32[]{:S(2)}, u32[]{:S(2)}) collective-permute-start(f32[16,1152]{1,0:T(8,128)S(1)} %convolution_add_fusion.2), channel_id=1, source_target_pairs={{0,16},{16,32},{32,48},{48,64},{64,80},{80,96},{96,112},{112,128},... | collective-permute-start | bytes 221192 | tf_op jit(solution)/shard_map/while/body/eval_jaxpr/ppermute | solution.py:9
  241.9 11.8 %collective-permute-start.1 = (f32[16,1152]{1,0:T(8,128)S(1)}, f32[16,1152]{1,0:T(8,128)S(1)}, u32[]{:S(2)}, u32[]{:S(2)}) collective-permute-start(f32[16,1152]{1,0:T(8,128)S(1)} %convolution_add_fusion.2), channel_id=1, source_target_pairs={{0,16},{16,32},{32,48},{48,64},{64,80},{80,96},{96,112},{112,128},... | collective-permute-start | bytes 221192 | tf_op jit(solution)/shard_map/while/body/eval_jaxpr/ppermute | solution.py:9
  257.0 11.8 %collective-permute-start.1 = (f32[16,1152]{1,0:T(8,128)S(1)}, f32[16,1152]{1,0:T(8,128)S(1)}, u32[]{:S(2)}, u32[]{:S(2)}) collective-permute-start(f32[16,1152]{1,0:T(8,128)S(1)} %convolution_add_fusion.2), channel_id=1, source_target_pairs={{0,16},{16,32},{32,48},{48,64},{64,80},{80,96},{96,112},{112,128},... | collective-permute-start | bytes 221192 | tf_op jit(solution)/shard_map/while/body/eval_jaxpr/ppermute | solution.py:9
  272.1 11.8 %collective-permute-start.1 = (f32[16,1152]{1,0:T(8,128)S(1)}, f32[16,1152]{1,0:T(8,128)S(1)}, u32[]{:S(2)}, u32[]{:S(2)}) collective-permute-start(f32[16,1152]{1,0:T(8,128)S(1)} %convolution_add_fusion.2), channel_id=1, source_target_pairs={{0,16},{16,32},{32,48},{48,64},{64,80},{80,96},{96,112},{112,128},... | collective-permute-start | bytes 221192 | tf_op jit(solution)/shard_map/while/body/eval_jaxpr/ppermute | solution.py:9
  287.2 11.8 %collective-permute-start.1 = (f32[16,1152]{1,0:T(8,128)S(1)}, f32[16,1152]{1,0:T(8,128)S(1)}, u32[]{:S(2)}, u32[]{:S(2)}) collective-permute-start(f32[16,1152]{1,0:T(8,128)S(1)} %convolution_add_fusion.2), channel_id=1, source_target_pairs={{0,16},{16,32},{32,48},{48,64},{64,80},{80,96},{96,112},{112,128},... | collective-permute-start | bytes 221192 | tf_op jit(solution)/shard_map/while/body/eval_jaxpr/ppermute | solution.py:9
  302.3 11.8 %collective-permute-start.1 = (f32[16,1152]{1,0:T(8,128)S(1)}, f32[16,1152]{1,0:T(8,128)S(1)}, u32[]{:S(2)}, u32[]{:S(2)}) collective-permute-start(f32[16,1152]{1,0:T(8,128)S(1)} %convolution_add_fusion.2), channel_id=1, source_target_pairs={{0,16},{16,32},{32,48},{48,64},{64,80},{80,96},{96,112},{112,128},... | collective-permute-start | bytes 221192 | tf_op jit(solution)/shard_map/while/body/eval_jaxpr/ppermute | solution.py:9
  317.5 11.8 %collective-permute-start.1 = (f32[16,1152]{1,0:T(8,128)S(1)}, f32[16,1152]{1,0:T(8,128)S(1)}, u32[]{:S(2)}, u32[]{:S(2)}) collective-permute-start(f32[16,1152]{1,0:T(8,128)S(1)} %convolution_add_fusion.2), channel_id=1, source_target_pairs={{0,16},{16,32},{32,48},{48,64},{64,80},{80,96},{96,112},{112,128},... | collective-permute-start | bytes 221192 | tf_op jit(solution)/shard_map/while/body/eval_jaxpr/ppermute | solution.py:9
  332.6 11.8 %collective-permute-start.1 = (f32[16,1152]{1,0:T(8,128)S(1)}, f32[16,1152]{1,0:T(8,128)S(1)}, u32[]{:S(2)}, u32[]{:S(2)}) collective-permute-start(f32[16,1152]{1,0:T(8,128)S(1)} %convolution_add_fusion.2), channel_id=1, source_target_pairs={{0,16},{16,32},{32,48},{48,64},{64,80},{80,96},{96,112},{112,128},... | collective-permute-start | bytes 221192 | tf_op jit(solution)/shard_map/while/body/eval_jaxpr/ppermute | solution.py:9
  347.7 11.8 %collective-permute-start.1 = (f32[16,1152]{1,0:T(8,128)S(1)}, f32[16,1152]{1,0:T(8,128)S(1)}, u32[]{:S(2)}, u32[]{:S(2)}) collective-permute-start(f32[16,1152]{1,0:T(8,128)S(1)} %convolution_add_fusion.2), channel_id=1, source_target_pairs={{0,16},{16,32},{32,48},{48,64},{64,80},{80,96},{96,112},{112,128},... | collective-permute-start | bytes 221192 | tf_op jit(solution)/shard_map/while/body/eval_jaxpr/ppermute | solution.py:9
  362.8 11.8 %collective-permute-start.1 = (f32[16,1152]{1,0:T(8,128)S(1)}, f32[16,1152]{1,0:T(8,128)S(1)}, u32[]{:S(2)}, u32[]{:S(2)}) collective-permute-start(f32[16,1152]{1,0:T(8,128)S(1)} %convolution_add_fusion.2), channel_id=1, source_target_pairs={{0,16},{16,32},{32,48},{48,64},{64,80},{80,96},{96,112},{112,128},... | collective-permute-start | bytes 221192 | tf_op jit(solution)/shard_map/while/body/eval_jaxpr/ppermute | solution.py:9
  377.9 11.8 %collective-permute-start.1 = (f32[16,1152]{1,0:T(8,128)S(1)}, f32[16,1152]{1,0:T(8,128)S(1)}, u32[]{:S(2)}, u32[]{:S(2)}) collective-permute-start(f32[16,1152]{1,0:T(8,128)S(1)} %convolution_add_fusion.2), channel_id=1, source_target_pairs={{0,16},{16,32},{32,48},{48,64},{64,80},{80,96},{96,112},{112,128},... | collective-permute-start | bytes 221192 | tf_op jit(solution)/shard_map/while/body/eval_jaxpr/ppermute | solution.py:9
  393.0 11.8 %collective-permute-start.1 = (f32[16,1152]{1,0:T(8,128)S(1)}, f32[16,1152]{1,0:T(8,128)S(1)}, u32[]{:S(2)}, u32[]{:S(2)}) collective-permute-start(f32[16,1152]{1,0:T(8,128)S(1)} %convolution_add_fusion.2), channel_id=1, source_target_pairs={{0,16},{16,32},{32,48},{48,64},{64,80},{80,96},{96,112},{112,128},... | collective-permute-start | bytes 221192 | tf_op jit(solution)/shard_map/while/body/eval_jaxpr/ppermute | solution.py:9
  408.1 11.8 %collective-permute-start.1 = (f32[16,1152]{1,0:T(8,128)S(1)}, f32[16,1152]{1,0:T(8,128)S(1)}, u32[]{:S(2)}, u32[]{:S(2)}) collective-permute-start(f32[16,1152]{1,0:T(8,128)S(1)} %convolution_add_fusion.2), channel_id=1, source_target_pairs={{0,16},{16,32},{32,48},{48,64},{64,80},{80,96},{96,112},{112,128},... | collective-permute-start | bytes 221192 | tf_op jit(solution)/shard_map/while/body/eval_jaxpr/ppermute | solution.py:9
  423.2 11.8 %collective-permute-start.1 = (f32[16,1152]{1,0:T(8,128)S(1)}, f32[16,1152]{1,0:T(8,128)S(1)}, u32[]{:S(2)}, u32[]{:S(2)}) collective-permute-start(f32[16,1152]{1,0:T(8,128)S(1)} %convolution_add_fusion.2), channel_id=1, source_target_pairs={{0,16},{16,32},{32,48},{48,64},{64,80},{80,96},{96,112},{112,128},... | collective-permute-start | bytes 221192 | tf_op jit(solution)/shard_map/while/body/eval_jaxpr/ppermute | solution.py:9
  438.3 11.8 %collective-permute-start.1 = (f32[16,1152]{1,0:T(8,128)S(1)}, f32[16,1152]{1,0:T(8,128)S(1)}, u32[]{:S(2)}, u32[]{:S(2)}) collective-permute-start(f32[16,1152]{1,0:T(8,128)S(1)} %convolution_add_fusion.2), channel_id=1, source_target_pairs={{0,16},{16,32},{32,48},{48,64},{64,80},{80,96},{96,112},{112,128},... | collective-permute-start | bytes 221192 | tf_op jit(solution)/shard_map/while/body/eval_jaxpr/ppermute | solution.py:9
  453.5 11.8 %collective-permute-start.1 = (f32[16,1152]{1,0:T(8,128)S(1)}, f32[16,1152]{1,0:T(8,128)S(1)}, u32[]{:S(2)}, u32[]{:S(2)}) collective-permute-start(f32[16,1152]{1,0:T(8,128)S(1)} %convolution_add_fusion.2), channel_id=1, source_target_pairs={{0,16},{16,32},{32,48},{48,64},{64,80},{80,96},{96,112},{112,128},... | collective-permute-start | bytes 221192 | tf_op jit(solution)/shard_map/while/body/eval_jaxpr/ppermute | solution.py:9
  468.6 11.8 %collective-permute-start.1 = (f32[16,1152]{1,0:T(8,128)S(1)}, f32[16,1152]{1,0:T(8,128)S(1)}, u32[]{:S(2)}, u32[]{:S(2)}) collective-permute-start(f32[16,1152]{1,0:T(8,128)S(1)} %convolution_add_fusion.2), channel_id=1, source_target_pairs={{0,16},{16,32},{32,48},{48,64},{64,80},{80,96},{96,112},{112,128},... | collective-permute-start | bytes 221192 | tf_op jit(solution)/shard_map/while/body/eval_jaxpr/ppermute | solution.py:9
  483.7 11.8 %collective-permute-start.1 = (f32[16,1152]{1,0:T(8,128)S(1)}, f32[16,1152]{1,0:T(8,128)S(1)}, u32[]{:S(2)}, u32[]{:S(2)}) collective-permute-start(f32[16,1152]{1,0:T(8,128)S(1)} %convolution_add_fusion.2), channel_id=1, source_target_pairs={{0,16},{16,32},{32,48},{48,64},{64,80},{80,96},{96,112},{112,128},... | collective-permute-start | bytes 221192 | tf_op jit(solution)/shard_map/while/body/eval_jaxpr/ppermute | solution.py:9
  498.8 11.9 %collective-permute-start.1 = (f32[16,1152]{1,0:T(8,128)S(1)}, f32[16,1152]{1,0:T(8,128)S(1)}, u32[]{:S(2)}, u32[]{:S(2)}) collective-permute-start(f32[16,1152]{1,0:T(8,128)S(1)} %convolution_add_fusion.2), channel_id=1, source_target_pairs={{0,16},{16,32},{32,48},{48,64},{64,80},{80,96},{96,112},{112,128},... | collective-permute-start | bytes 221192 | tf_op jit(solution)/shard_map/while/body/eval_jaxpr/ppermute | solution.py:9
  514.0 11.8 %collective-permute-start.1 = (f32[16,1152]{1,0:T(8,128)S(1)}, f32[16,1152]{1,0:T(8,128)S(1)}, u32[]{:S(2)}, u32[]{:S(2)}) collective-permute-start(f32[16,1152]{1,0:T(8,128)S(1)} %convolution_add_fusion.2), channel_id=1, source_target_pairs={{0,16},{16,32},{32,48},{48,64},{64,80},{80,96},{96,112},{112,128},... | collective-permute-start | bytes 221192 | tf_op jit(solution)/shard_map/while/body/eval_jaxpr/ppermute | solution.py:9
  (34 other events, 442.8 us)
where the time goes:
time: 612 us; the launch traced here: 602 us
  waiting for transfers between devices  304 us (50%)
  starting transfers between devices  134 us (22%)
  blocking collectives  111 us (18%)
  matrix products  45.2 us (7%)
    ppermute x64, waiting for transfers between devices, from_behind(): lax.ppermute(array, axis, [(i, (i + by) % peers) for i in range(peers)])  304 us
    ppermute x64, starting transfers between devices, from_behind(): lax.ppermute(array, axis, [(i, (i + by) % peers) for i in range(peers)])  134 us
    unnamed x1, blocking collectives  72 us
    all_gather x1, blocking collectives, local(): group_block = lax.all_gather(texts, 'grp', axis=0, tiled=True)  38.9 us
    dot_general x32, matrix products, tile_terms(): lax.dot_general(images, text_block, (((1,), (1,)), ((), ())), preferred_e...  34.7 us
  transfers between devices with their start and end apart: 64, of which 63 were waited for; matrix products, arithmetic and copies ran while one was open for 7% of the time, Pallas kernels for 0%

commit v1 on v0

v1 whole, which is shorter than its diff:
```python
import jax
import jax.numpy as jnp
from jax import lax
from jax.sharding import Mesh
from jax.sharding import PartitionSpec as P

WIDE = ("far", "near")


def swap_cores(array):
    return lax.ppermute(array, "core", [(0, 1), (1, 0)])


def exchange(array):
    return lax.all_to_all(array, WIDE, 0, 0, tiled=True)


def coefficients(images, labels, block, columns, factor, offset, weight):
    logits = (
        factor
        * lax.dot_general(
            images, block, (((1,), (1,)), ((), ())), preferred_element_type=jnp.float32
        )
        + offset
    )
    pair_sign = jnp.where(labels[:, None] == columns[None, :], 1.0, -1.0).astype(jnp.float32)
    return (-pair_sign * jax.nn.sigmoid(-pair_sign * logits) * weight).astype(jnp.bfloat16)


def text_part(coefficient, images):
    return lax.dot_general(
        coefficient, images, (((0,), (0,)), ((), ())), preferred_element_type=jnp.float32
    )


def local(images, texts, labels, log_scale, bias, loss_scale):
    far, cores, near = (lax.axis_size(name) for name in ("far", "core", "near"))
    core = lax.axis_index("core")
    factor = jnp.exp(log_scale[0])
    offset = bias[0]
    weight = factor * loss_scale[0] / (images.shape[0] * far * cores * near)
    shared = far * near

    place = jnp.arange(shared, dtype=jnp.int32)
    first = place // near * (cores * near) + place % near
    columns_mine = first + core * near
    columns_other = first + (1 - core) * near

    with jax.named_scope("gather_texts"):
        mine = exchange(jnp.broadcast_to(texts, (shared, texts.shape[1])))
        other = swap_cores(mine)

    with jax.named_scope("coefficients"):
        coef_mine = coefficients(images, labels, mine, columns_mine, factor, offset, weight)
        coef_other = coefficients(images, labels, other, columns_other, factor, offset, weight)

    with jax.named_scope("text_grad"):
        given = swap_cores(text_part(coef_other, images).astype(jnp.bfloat16))
        kept = text_part(coef_mine, images)
        pair = (kept + given.astype(jnp.float32)).astype(jnp.bfloat16)
        parts = exchange(pair)
        text_grad = jnp.sum(parts.astype(jnp.float32), axis=0, keepdims=True)

    with jax.named_scope("image_grad"):
        image_grad = jnp.dot(
            jnp.concatenate([coef_mine, coef_other], 1),
            jnp.concatenate([mine, other], 0),
            preferred_element_type=jnp.float32,
        )
    return (image_grad.astype(jnp.bfloat16), text_grad.astype(jnp.bfloat16))


def solution(mesh):
    blk, grp = mesh.devices.shape
    fine = Mesh(mesh.devices.reshape(blk // 2, 2, grp), ("far", "core", "near"))
    rows = ("far", "core", "near")
    placed = (P(rows, None), P(rows, None), P(rows), P(), P(), P())
    return jax.shard_map(
        local,
        mesh=fine,
        in_specs=placed,
        out_specs=(P(rows, None), P(rows, None)),
        check_vma=False,
    )
```

time: 612 us -> 102 us (0.17); the launches traced: 602 us -> 102 us
  waiting for transfers between devices: 304 us -> 23 us
  starting transfers between devices: 134 us -> 13 us
  blocking collectives: 111 us -> 44.9 us
  matrix products: 45.2 us -> 4.28 us
  other arithmetic: 0.12 us -> 7.13 us
    ppermute x64 -> x2, waiting for transfers between devices: 304 us -> 0.71 us  [swap_cores(): return lax.ppermute(array, 'core', [(0, 1), (1, 0)])]
    ppermute x64 -> x2, starting transfers between devices: 134 us -> 4.5 us  [swap_cores(): return lax.ppermute(array, 'core', [(0, 1), (1, 0)])]
    unnamed x1 -> x0, blocking collectives: 72 us -> none
    all_to_all x0 -> x1, blocking collectives: none -> 44.9 us  [exchange(): return lax.all_to_all(array, WIDE, 0, 0, tiled=True)]
    dot_general x65 -> x5, matrix products: 45.2 us -> 4.28 us  [the longest x1 1.89 us: local(): jnp.dot(jnp.concatenate([coef_mine, coef_other], 1), jnp.concatenate([min...]
    all_gather x1 -> x0, blocking collectives: 38.9 us -> none  [local(): group_block = lax.all_gather(texts, 'grp', axis=0, tiled=True)]
    all_to_all x0 -> x1, waiting for transfers between devices: none -> 22.3 us  [exchange(): return lax.all_to_all(array, WIDE, 0, 0, tiled=True)]
    all_to_all x0 -> x1, starting transfers between devices: none -> 8.51 us  [exchange(): return lax.all_to_all(array, WIDE, 0, 0, tiled=True)]
  transfers between devices with their start and end apart: 64 -> 3, of which waited for: 63 -> 2; matrix products, arithmetic and copies ran while one was open for 7% -> 3% of each run, Pallas kernels for 0% -> 0%
where the time goes in v1:
time: 102 us
  blocking collectives  44.9 us (44%)
  waiting for transfers between devices  23 us (23%)
  starting transfers between devices  13 us (13%)
  other arithmetic  7.13 us (7%)
  local copies, waits for them, and re-layouts  6.71 us (7%)
  matrix products  4.28 us (4%)
  between operations  2.8 us (3%)
    all_to_all x1, blocking collectives, exchange(): return lax.all_to_all(array, WIDE, 0, 0, tiled=True)  44.9 us
    all_to_all x1, waiting for transfers between devices, exchange(): return lax.all_to_all(array, WIDE, 0, 0, tiled=True)  22.3 us
    all_to_all x1, starting transfers between devices, exchange(): return lax.all_to_all(array, WIDE, 0, 0, tiled=True)  8.51 us
    unnamed x17, local copies, waits for them, and re-layouts  4.99 us
    ppermute x2, starting transfers between devices, swap_cores(): return lax.ppermute(array, 'core', [(0, 1), (1, 0)])  4.5 us
    broadcast_in_dim x1, other arithmetic, local(): mine = exchange(jnp.broadcast_to(texts, (shared, texts.shape[1])))  4.21 us
  transfers between devices with their start and end apart: 3, of which 2 were waited for; matrix products, arithmetic and copies ran while one was open for 3% of the time, Pallas kernels for 0%

profile of v1, /device:TPU:6, one launch (start us, length us, event | category | flops | bytes accessed | tf_op | source)
XLA Modules:
  0.0 101.8 jit_solution(895358923834111343)
XLA Ops:
  0.6 0.0 copy-start
  0.6 0.8 reduce.2
  1.5 0.6 broadcast_in_dim.22
  2.1 0.5 broadcast.111
  2.6 4.2 %reduce.3 = bf16[256,1152]{1,0:T(8,128)(2,1)S(1)} reduce(bf16[256,1,1152]{2,1,0:T(2,128)(2,1)S(1)} %broadcast_in_dim.22, bf16[]{:T(256)} %broadcast.111), dimensions={1}, to_apply=%broadcast_in_dim.22.reduce_sub_computation | reduce | bytes 1179650 | tf_op jit(solution)/shard_map/gather_texts/broadcast_in_dim | solution.py:50
  6.8 0.6 reshape.51
  7.4 44.9 %all_to_all.18 = bf16[256,2,576]{2,1,0:T(2,128)(2,1)S(1)} all-to-all(bf16[256,2,576]{2,1,0:T(2,128)(2,1)S(1)} %reshape.51), channel_id=1, replica_groups=mesh['far'=16,'core'=2,'near'=16] {'far','near'}, dimensions={0} | all-to-all | bytes 1179648 | tf_op jit(solution)/shard_map/gather_texts/all_to_all | solution.py:15
  52.3 1.0 reshape.52
  53.3 0.0 copy-start.5
  53.3 0.1 copy.11
  53.4 0.0 copy-start.1
  53.4 1.9 %collective-permute-start = (bf16[256,1152]{1,0:T(8,128)(2,1)S(1)}, bf16[256,1152]{1,0:T(8,128)(2,1)S(1)}, u32[]{:S(2)}, u32[]{:S(2)}) collective-permute-start(bf16[256,1152]{1,0:T(8,128)(2,1)S(1)} %bitcast.19), channel_id=1, source_target_pairs={{0,16},{16,0},{1,17},{17,1},{2,18},{18,2},{3,19},{19,3},{4,20},{20... | collective-permute-start | bytes 1769480 | tf_op jit(solution)/shard_map/gather_texts/ppermute | solution.py:11
  57.3 0.0 collective-permute-done
  57.3 0.0 copy-start.3
  57.4 0.8 copy-done.3
  58.2 0.0 copy-done
  58.2 0.7 fusion.16
  58.9 0.5 convolution_convert_fusion.1
  59.4 2.6 %collective-permute-start.1 = (bf16[256,1152]{1,0:T(8,128)(2,1)S(1)}, bf16[256,1152]{1,0:T(8,128)(2,1)S(1)}, u32[]{:S(2)}, u32[]{:S(2)}) collective-permute-start(bf16[256,1152]{1,0:T(8,128)(2,1)S(1)} %convolution_convert_fusion.1), channel_id=1, source_target_pairs={{0,16},{16,0},{1,17},{17,1},{2,18},{18,2},{3,19},{19,3},{4,20},{20... | collective-permute-start | bytes 1769480 | tf_op jit(solution)/shard_map/text_grad/ppermute | solution.py:11
  62.0 0.7 fusion.17
  62.7 0.7 collective-permute-done.1
  63.4 0.5 fusion.21
  63.9 1.0 %reduce.4 = bf16[256,1152]{1,0:T(8,128)(2,1)S(1)} reduce(bf16[256,1,1152]{2,0,1:T(8,128)(2,1)S(1)} %fusion.21, bf16[]{:T(256)} %broadcast.111), dimensions={1}, to_apply=%copy.8.reduce_sub_computation | reduce | bytes 1179650 | tf_op jit(solution)/shard_map/text_grad/all_to_all | solution.py:15
  65.0 1.5 %reshape.53 = bf16[256,2,576]{2,1,0:T(2,128)(2,1)} reshape(bf16[256,1152]{1,0:T(8,128)(2,1)S(1)} %reduce.4) | data formatting | bytes 1179648
  66.4 8.5 %all-to-all-start.1 = ((bf16[256,2,576]{2,1,0:T(2,128)(2,1)}), bf16[256,2,576]{2,1,0:T(2,128)(2,1)S(1)}, u32[]{:S(2)}, u32[]{:S(2)}) async-start(bf16[256,2,576]{2,1,0:T(2,128)(2,1)} %reshape.53), calls=%async_computation.1 | async-start | bytes 1310720 | tf_op jit(solution)/shard_map/text_grad/all_to_all | solution.py:15
  75.0 0.0 copy-done.2
  75.0 0.0 copy-done.4
  75.0 1.9 %convolution_convert_fusion = bf16[512,1152]{1,0:T(8,128)(2,1)} fusion(bf16[256,1152]{1,0:T(8,128)(2,1)S(1)} %copy-done.4, bf16[256,1152]{1,0:T(8,128)(2,1)S(1)} %bitcast.21, bf16[512,256]{0,1:T(8,128)(2,1)S(1)} %fusion.16, bf16[512,256]{0,1:T(8,128)(2,1)S(1)} %fusion.17), kind=kOutput, calls=%fused_computation | convolution fusion | flops 607977472 | bytes 2883584 | tf_op jit(solution)/shard_map/image_grad/dot_general | solution.py:65
  76.9 22.3 %all-to-all-done.1 = bf16[256,2,576]{2,1,0:T(2,128)(2,1)S(1)} async-done(((bf16[256,2,576]{2,1,0:T(2,128)(2,1)}), bf16[256,2,576]{2,1,0:T(2,128)(2,1)S(1)}, u32[]{:S(2)}, u32[]{:S(2)}) %all-to-all-start.1) | async-done | bytes 589856 | tf_op jit(solution)/shard_map/text_grad/all_to_all | solution.py:15
  99.2 1.0 reshape.54
  100.2 1.1 %reduce_sum.12 = bf16[1152]{0:T(1024)(128)(2,1)S(1)} reduce(bf16[256,1,1152]{2,1,0:T(2,128)(2,1)S(1)} %reshape.54, bf16[]{:T(256)} %constant.52.clone.1), dimensions={0,1}, to_apply=%region_0.1 | reduce | flops 293760 | bytes 592130 | tf_op jit(solution)/shard_map/text_grad/reduce_sum | solution.py:62
  101.2 0.6 convert_element_type.38
  (6 shorter events, 0.0 us)
Async XLA Ops:
  0.6 57.5 %copy-start = (bf16[512,1152]{1,0:T(8,128)(2,1)S(1)}, bf16[512,1152]{1,0:T(8,128)(2,1)}, u32[]{:S(2)}) copy-start(bf16[512,1152]{1,0:T(8,128)(2,1)} %param.6) | copy-start | bytes 3538948
  53.3 4.9 %copy-start.5 = (s32[512]{0:T(512)S(1)}, s32[512]{0:T(512)}, u32[]{:S(2)}) copy-start(s32[512]{0:T(512)} %param.8) | copy-start | bytes 6148
  53.4 8.6 %copy-start.1 = (bf16[256,1,1152]{2,0,1:T(8,128)(2,1)}, bf16[256,1,1152]{2,0,1:T(8,128)(2,1)S(1)}, u32[]{:S(2)}) copy-start(bf16[256,1,1152]{2,0,1:T(8,128)(2,1)S(1)} %copy.11) | copy-start | bytes 1769476
  53.4 3.9 %collective-permute-start = (bf16[256,1152]{1,0:T(8,128)(2,1)S(1)}, bf16[256,1152]{1,0:T(8,128)(2,1)S(1)}, u32[]{:S(2)}, u32[]{:S(2)}) collective-permute-start(bf16[256,1152]{1,0:T(8,128)(2,1)S(1)} %bitcast.19), channel_id=1, source_target_pairs={{0,16},{16,0},{1,17},{17,1},{2,18},{18,2},{3,19},{19,3},{4,20},{20... | collective-permute-start | bytes 1769480 | tf_op jit(solution)/shard_map/gather_texts/ppermute | solution.py:11
  57.3 0.8 copy-start.3
  59.4 4.0 %collective-permute-start.1 = (bf16[256,1152]{1,0:T(8,128)(2,1)S(1)}, bf16[256,1152]{1,0:T(8,128)(2,1)S(1)}, u32[]{:S(2)}, u32[]{:S(2)}) collective-permute-start(bf16[256,1152]{1,0:T(8,128)(2,1)S(1)} %convolution_convert_fusion.1), channel_id=1, source_target_pairs={{0,16},{16,0},{1,17},{17,1},{2,18},{18,2},{3,19},{19,3},{4,20},{20... | collective-permute-start | bytes 1769480 | tf_op jit(solution)/shard_map/text_grad/ppermute | solution.py:11
  65.0 10.0 %copy-start.2 = (bf16[256,1,1152]{2,0,1:T(8,128)(2,1)S(1)}, bf16[256,1,1152]{2,0,1:T(8,128)(2,1)}, u32[]{:S(2)}) copy-start(bf16[256,1,1152]{2,0,1:T(8,128)(2,1)} %copy-done.1) | copy-start | bytes 1769476
  66.4 8.5 %copy-start.4 = (bf16[256,1152]{1,0:T(8,128)(2,1)S(1)}, bf16[256,1152]{1,0:T(8,128)(2,1)}, u32[]{:S(2)}) copy-start(bf16[256,1152]{1,0:T(8,128)(2,1)} %copy-done.3) | copy-start | bytes 1769476
  66.4 32.7 %all-to-all-start.1 = ((bf16[256,2,576]{2,1,0:T(2,128)(2,1)}), bf16[256,2,576]{2,1,0:T(2,128)(2,1)S(1)}, u32[]{:S(2)}, u32[]{:S(2)}) async-start(bf16[256,2,576]{2,1,0:T(2,128)(2,1)} %reshape.53), calls=%async_computation.1 | async-start | bytes 1310720 | tf_op jit(solution)/shard_map/text_grad/all_to_all | solution.py:15

commit v2 on v1

v2 whole, which is shorter than its diff:
```python
import jax
import jax.numpy as jnp
from jax import lax
from jax.experimental import pallas as pl
from jax.experimental.pallas import tpu as pltpu
from jax.sharding import Mesh
from jax.sharding import PartitionSpec as P

WIDE = ("far", "zl", "x")
IN_PIECES = 2
OUT_PIECES = 4
HBM = pl.BlockSpec(memory_space=pltpu.HBM)
VMEM = pl.BlockSpec(memory_space=pltpu.VMEM)
SMEM = pl.BlockSpec(memory_space=pltpu.SMEM)
PARAMS = pltpu.CompilerParams(vmem_limit_bytes=24 << 20)


def swap_cores(*arrays):
    return [lax.ppermute(array, "core", [(0, 1), (1, 0)]) for array in arrays]


def exchange(array):
    return lax.all_to_all(array, WIDE, 0, 0, tiled=True)


def dot(left, right, along):
    return lax.dot_general(
        left, right, ((along[:1], along[1:]), ((), ())), preferred_element_type=jnp.float32
    )


def put(space, *arrays):
    return [pltpu.with_memory_space_constraint(array, space) for array in arrays]


def cost(flops, moved, exps=0):
    return pl.CostEstimate(flops=flops, bytes_accessed=moved, transcendentals=exps)


def repeat_kernel(row, out):
    width = out.shape[2]
    values = row[...].astype(jnp.float32)
    halves = jnp.concatenate([values[:, :width], values[:, width:]], 0).astype(out.dtype)
    out[...] = jnp.broadcast_to(halves[None], out.shape)


def split_kernel(whole, *refs):
    *pieces, held, sems, out_sems = refs
    size = pieces[0].shape[0]
    loads, stores = [], []
    for index, piece in enumerate(pieces):
        span = pl.ds(index * size, size)
        loads.append(pltpu.make_async_copy(whole.at[span], held.at[index], sems.at[index]))
        stores.append(pltpu.make_async_copy(held.at[index], piece, out_sems.at[index]))
    for load in loads:
        load.start()
    for load, store in zip(loads, stores):
        load.wait()
        store.start()
    for store in stores:
        store.wait()


def coefficient_kernel(scalars, columns, halves, labels, other_labels, images, *refs):
    *others, block_out, coef_out, other_coef_out, part = refs[:-6]
    own, block, coef, other_coef, sem, out_sems = refs[-6:]
    load = pltpu.make_async_copy(images, own, sem)
    load.start()
    factor, offset, weight = scalars[0], scalars[1], scalars[2]
    block[...] = halves[...].reshape(block.shape)
    stores = [pltpu.make_async_copy(block, block_out, out_sems.at[0])]
    stores[0].start()
    load.wait()

    def piece(frames, paired):
        logits = factor * dot(block[...], frames, (1, 1)) + offset
        pair_sign = jnp.where(paired == columns[...], 1.0, -1.0).astype(jnp.float32)
        value = -pair_sign * jax.nn.sigmoid(-pair_sign * logits) * weight
        value = value.astype(jnp.bfloat16)
        return value, dot(value, frames, (1, 0))

    coef[...], total = piece(own[...], labels[...])
    stores.append(pltpu.make_async_copy(coef, coef_out, out_sems.at[1]))
    stores[1].start()
    for index, frames in enumerate(others):
        size = frames.shape[0]
        span = pl.ds(index * size, size)
        other_coef[:, span], term = piece(frames[...], other_labels[:, span])
        total = total + term
    stores.append(pltpu.make_async_copy(other_coef, other_coef_out, out_sems.at[2]))
    stores[2].start()
    width = part.shape[2]
    part[:, 0, :] = total[:, :width].astype(part.dtype)
    part[:, 1, :] = total[:, width:].astype(part.dtype)
    for store in stores:
        store.wait()


def partial_kernel(coef_in, block_in, *refs):
    *outs, coef, block, held, in_sems, sems = refs
    size = outs[0].shape[0]
    loads = [
        pltpu.make_async_copy(coef_in, coef, in_sems.at[0]),
        pltpu.make_async_copy(block_in, block, in_sems.at[1]),
    ]
    for load in loads:
        load.start()
    for load in loads:
        load.wait()
    stores = []
    for index, out in enumerate(outs):
        held[index] = dot(coef[:, pl.ds(index * size, size)], block[...], (0, 0))
        stores.append(pltpu.make_async_copy(held.at[index], out, sems.at[index]))
        stores[-1].start()
    for store in stores:
        store.wait()


def image_kernel(coef_in, block_in, *refs):
    *given, out, coef, block, held, result, in_sems, sems, out_sems = refs
    size = given[0].shape[0]
    loads = [
        pltpu.make_async_copy(coef_in, coef, in_sems.at[0]),
        pltpu.make_async_copy(block_in, block, in_sems.at[1]),
    ]
    copies = [
        pltpu.make_async_copy(source, held.at[index], sems.at[index])
        for index, source in enumerate(given)
    ]
    for load in loads + copies:
        load.start()
    for load in loads:
        load.wait()
    stores = []
    for index, copy in enumerate(copies):
        span = pl.ds(index * size, size)
        share = dot(coef[:, span], block[...], (0, 0))
        copy.wait()
        result[index] = (share + held[index]).astype(result.dtype)
        stores.append(pltpu.make_async_copy(result.at[index], out.at[span], out_sems.at[index]))
        stores[-1].start()
    for store in stores:
        store.wait()


def local(images, texts, labels, log_scale, bias, loss_scale):
    far, cores, x, zl = (lax.axis_size(name) for name in ("far", "core", "x", "zl"))
    core = lax.axis_index("core")
    rows = images.shape[0]
    width = texts.shape[1]
    shared = far * x * zl
    factor = jnp.exp(log_scale[0])
    weight = factor * loss_scale[0] / (rows * shared * cores)
    scalars = jnp.stack([factor, bias[0], weight])
    flops = 2 * shared * rows * width

    place = jnp.arange(shared, dtype=jnp.int32)
    columns = place // (x * zl) * (cores * x * zl) + core * x * zl
    columns = columns + place % x * zl + place // x % zl

    with jax.named_scope("gather_texts"):
        halves = pl.pallas_call(
            repeat_kernel,
            out_shape=pltpu.VMEM((shared, 2, width // 2), texts.dtype),
            in_specs=[VMEM],
            out_specs=VMEM,
            compiler_params=PARAMS,
        )(texts)
        halves = exchange(halves)

    with jax.named_scope("swap_images"):
        pieces = pl.pallas_call(
            split_kernel,
            out_shape=[pltpu.HBM((rows // IN_PIECES, width), images.dtype)] * IN_PIECES,
            in_specs=[HBM],
            out_specs=[HBM] * IN_PIECES,
            scratch_shapes=[
                pltpu.VMEM((IN_PIECES, rows // IN_PIECES, width), images.dtype),
                pltpu.SemaphoreType.DMA((IN_PIECES,)),
                pltpu.SemaphoreType.DMA((IN_PIECES,)),
            ],
            compiler_params=PARAMS,
            cost_estimate=cost(0, 4 * rows * width),
        )(*put(pltpu.HBM, images))
        *others, labels_other = swap_cores(*pieces, labels)

    with jax.named_scope("coefficients"):
        block, coef, coef_other, part = pl.pallas_call(
            coefficient_kernel,
            out_shape=(
                pltpu.HBM((shared, width), jnp.bfloat16),
                pltpu.HBM((shared, rows), jnp.bfloat16),
                pltpu.HBM((shared, rows), jnp.bfloat16),
                pltpu.VMEM((shared, 2, width // 2), jnp.bfloat16),
            ),
            in_specs=[SMEM] + [VMEM] * 4 + [HBM] + [VMEM] * IN_PIECES,
            out_specs=(HBM, HBM, HBM, VMEM),
            scratch_shapes=[
                pltpu.VMEM((rows, width), jnp.bfloat16),
                pltpu.VMEM((shared, width), jnp.bfloat16),
                pltpu.VMEM((shared, rows), jnp.bfloat16),
                pltpu.VMEM((shared, rows), jnp.bfloat16),
                pltpu.SemaphoreType.DMA,
                pltpu.SemaphoreType.DMA((3,)),
            ],
            compiler_params=PARAMS,
            cost_estimate=cost(4 * flops, 4 * rows * width, 2 * shared * rows),
        )(
            scalars,
            columns[:, None],
            *put(pltpu.VMEM, halves),
            labels[None, :],
            labels_other[None, :],
            *put(pltpu.HBM, images),
            *put(pltpu.VMEM, *others),
        )

    with jax.named_scope("text_grad"):
        parts = exchange(part)
        text_grad = jnp.sum(parts.astype(jnp.float32), axis=0).reshape(1, width)

    with jax.named_scope("image_grad"):
        size = rows // OUT_PIECES
        given = pl.pallas_call(
            partial_kernel,
            out_shape=[pltpu.HBM((size, width), jnp.float32)] * OUT_PIECES,
            in_specs=[HBM, HBM],
            out_specs=[HBM] * OUT_PIECES,
            scratch_shapes=[
                pltpu.VMEM((shared, rows), jnp.bfloat16),
                pltpu.VMEM((shared, width), jnp.bfloat16),
                pltpu.VMEM((OUT_PIECES, size, width), jnp.float32),
                pltpu.SemaphoreType.DMA((2,)),
                pltpu.SemaphoreType.DMA((OUT_PIECES,)),
            ],
            compiler_params=PARAMS,
            cost_estimate=cost(flops, 4 * rows * width),
        )(*put(pltpu.HBM, coef_other, block))
        image_grad = pl.pallas_call(
            image_kernel,
            out_shape=jax.ShapeDtypeStruct((rows, width), jnp.bfloat16),
            in_specs=[HBM] * (2 + OUT_PIECES),
            out_specs=HBM,
            scratch_shapes=[
                pltpu.VMEM((shared, rows), jnp.bfloat16),
                pltpu.VMEM((shared, width), jnp.bfloat16),
                pltpu.VMEM((OUT_PIECES, size, width), jnp.float32),
                pltpu.VMEM((OUT_PIECES, size, width), jnp.bfloat16),
                pltpu.SemaphoreType.DMA((2,)),
                pltpu.SemaphoreType.DMA((OUT_PIECES,)),
                pltpu.SemaphoreType.DMA((OUT_PIECES,)),
            ],
            compiler_params=PARAMS,
            cost_estimate=cost(flops, 6 * rows * width),
        )(*put(pltpu.HBM, coef, block), *swap_cores(*given))
    return (image_grad, text_grad.astype(jnp.bfloat16))


def solution(mesh):
    blk, grp = mesh.devices.shape
    rows = ("far", "core", "x", "zl")
    fine = Mesh(mesh.devices.reshape(blk // 2, 2, 4, grp // 4), rows)
    placed = (P(rows, None), P(rows, None), P(rows), P(), P(), P())
    return jax.shard_map(
        local,
        mesh=fine,
        in_specs=placed,
        out_specs=(P(rows, None), P(rows, None)),
        check_vma=False,
    )
```

time: 102 us -> 86.2 us (0.85); the launches traced: 102 us -> 84.8 us
  blocking collectives: 44.9 us -> 0 us
  starting transfers between devices: 13 us -> 46.2 us
  Pallas kernels: 0 us -> 15.5 us
  other arithmetic: 7.13 us -> 0.77 us
  local copies, waits for them, and re-layouts: 6.71 us -> 1.37 us
  waiting for transfers between devices: 23 us -> 18.3 us
  matrix products: 4.28 us -> 0 us
    all_to_all x1 -> x0, blocking collectives: 44.9 us -> none  [exchange(): return lax.all_to_all(array, WIDE, 0, 0, tiled=True)]
    all_to_all x1 -> x2, starting transfers between devices: 8.51 us -> 31.3 us  [exchange(): return lax.all_to_all(array, WIDE, 0, 0, tiled=True)]
    pallas_call x0 -> x5, Pallas kernels: none -> 15.5 us  [the longest x1 6.3 us: local(): pl.pallas_call(coefficient_kernel, out_shape=(pltpu.HBM((shared, width),...]
    ppermute x2 -> x7, starting transfers between devices: 4.5 us -> 14.9 us  [swap_cores(): return [lax.ppermute(array, 'core', [(0, 1), (1, 0)]) for array in arrays]]
    all_to_all x1 -> x2, waiting for transfers between devices: 22.3 us -> 16.5 us  [exchange(): return lax.all_to_all(array, WIDE, 0, 0, tiled=True)]
    unnamed x17 -> x4, local copies, waits for them, and re-layouts: 4.99 us -> 0.68 us
    dot_general x5 -> x0, matrix products: 4.28 us -> none  [the longest x1 1.89 us: local(): jnp.dot(jnp.concatenate([coef_mine, coef_other], 1), jnp.concatenate([min...]
    broadcast_in_dim x1 -> x0, other arithmetic: 4.21 us -> none  [local(): mine = exchange(jnp.broadcast_to(texts, (shared, texts.shape[1])))]
  transfers between devices with their start and end apart: 3 -> 9, of which waited for: 2 -> 3; matrix products, arithmetic and copies ran while one was open for 3% -> 0% of each run, Pallas kernels for 0% -> 10%
where the time goes in v2:
time: 86.2 us; the launch traced here: 84.8 us
  starting transfers between devices  46.2 us (54%)
  waiting for transfers between devices  18.3 us (21%)
  Pallas kernels  15.5 us (18%)
  between operations  2.78 us (3%)
  local copies, waits for them, and re-layouts  1.37 us (2%)
    all_to_all x2, starting transfers between devices, exchange(): return lax.all_to_all(array, WIDE, 0, 0, tiled=True)  31.3 us
    all_to_all x2, waiting for transfers between devices, exchange(): return lax.all_to_all(array, WIDE, 0, 0, tiled=True)  16.5 us
    ppermute x7, starting transfers between devices, swap_cores(): return [lax.ppermute(array, 'core', [(0, 1), (1, 0)]) for array in arrays]  14.9 us
    pallas_call x1, Pallas kernels, local(): pl.pallas_call(coefficient_kernel, out_shape=(pltpu.HBM((shared, width),...  6.3 us
    pallas_call x1, Pallas kernels, local(): pl.pallas_call(image_kernel, out_shape=jax.ShapeDtypeStruct((rows, width)...  3.18 us
    pallas_call x1, Pallas kernels, local(): pl.pallas_call(partial_kernel, out_shape=[pltpu.HBM((size, width), jnp.fl...  2.9 us
    pallas_call x1, Pallas kernels, local(): pl.pallas_call(split_kernel, out_shape=[pltpu.HBM((rows // IN_PIECES, wid...  2.13 us
    ppermute x7, waiting for transfers between devices, swap_cores(): return [lax.ppermute(array, 'core', [(0, 1), (1, 0)]) for array in arrays]  1.8 us
  transfers between devices with their start and end apart: 9, of which 3 were waited for; matrix products, arithmetic and copies ran while one was open for 0% of the time, Pallas kernels for 10%

profile of v2, /device:TPU:6, one launch (start us, length us, event | category | flops | bytes accessed | tf_op | source)
XLA Modules:
  0.0 84.8 jit_solution(12503385736239635473)
XLA Ops:
  0.6 0.0 copy-start
  0.6 0.7 copy-done
  1.3 1.0 %gather_texts.1 = bf16[256,2,576]{2,1,0:T(2,128)(2,1)} custom-call(bf16[1,1152]{1,0:T(2,128)(2,1)S(1)} %copy-done), custom_call_target="tpu_custom_call" | custom-call | tf_op jit(solution)/shard_map/gather_texts/pallas_call | solution.py:162
  2.3 0.0 copy-start.1
  2.3 21.5 %all-to-all-start = ((bf16[256,2,576]{2,1,0:T(2,128)(2,1)}), bf16[256,2,576]{2,1,0:T(2,128)(2,1)S(1)}, u32[]{:S(2)}, u32[]{:S(2)}) async-start(bf16[256,2,576]{2,1,0:T(2,128)(2,1)} %gather_texts.1), calls=%async_computation | async-start | bytes 1310720 | tf_op jit(solution)/shard_map/gather_texts/all_to_all | solution.py:23
  23.8 2.1 %swap_images.1 = (bf16[256,1152]{1,0:T(8,128)(2,1)}, bf16[256,1152]{1,0:T(8,128)(2,1)}) custom-call(bf16[512,1152]{1,0:T(8,128)(2,1)} %images.1), custom_call_target="tpu_custom_call" | custom-call | bytes 2359296 | tf_op jit(solution)/shard_map/swap_images/pallas_call | solution.py:172
  25.9 1.9 %collective-permute-start.1 = (bf16[256,1152]{1,0:T(8,128)(2,1)}, bf16[256,1152]{1,0:T(8,128)(2,1)S(1)}, u32[]{:S(2)}, u32[]{:S(2)}) collective-permute-start(bf16[256,1152]{1,0:T(8,128)(2,1)} %get-tuple-element.12), channel_id=1, source_target_pairs={{0,16},{16,0},{1,17},{17,1},{2,18},{18,2},{3,19},{19,3},{4,20},{20... | collective-permute-start | bytes 1769480 | tf_op jit(solution)/shard_map/swap_images/ppermute | solution.py:19
  27.9 2.4 %collective-permute-start.2 = (bf16[256,1152]{1,0:T(8,128)(2,1)}, bf16[256,1152]{1,0:T(8,128)(2,1)S(1)}, u32[]{:S(2)}, u32[]{:S(2)}) collective-permute-start(bf16[256,1152]{1,0:T(8,128)(2,1)} %get-tuple-element.13), channel_id=1, source_target_pairs={{0,16},{16,0},{1,17},{17,1},{2,18},{18,2},{3,19},{19,3},{4,20},{20... | collective-permute-start | bytes 1769480 | tf_op jit(solution)/shard_map/swap_images/ppermute | solution.py:19
  30.3 0.0 copy-done.1
  30.3 1.9 %collective-permute-start = (s32[512]{0:T(512)S(1)}, s32[512]{0:T(512)S(1)}, u32[]{:S(2)}, u32[]{:S(2)}) collective-permute-start(s32[512]{0:T(512)S(1)} %copy-done.1), channel_id=1, source_target_pairs={{0,16},{16,0},{1,17},{17,1},{2,18},{18,2},{3,19},{19,3},{4,20},{20... | collective-permute-start | bytes 6152 | tf_op jit(solution)/shard_map/swap_images/ppermute | solution.py:19
  34.2 0.1 fusion.3.columns
  34.3 0.1 pad_maximum_fusion.scalars
  34.3 0.0 collective-permute-done
  34.3 0.0 collective-permute-done.1.refs_0_
  34.4 0.0 collective-permute-done.2.refs_1_
  34.4 11.8 %all-to-all-done.halves = bf16[256,2,576]{2,1,0:T(2,128)(2,1)S(1)} async-done(((bf16[256,2,576]{2,1,0:T(2,128)(2,1)}), bf16[256,2,576]{2,1,0:T(2,128)(2,1)S(1)}, u32[]{:S(2)}, u32[]{:S(2)}) %all-to-all-start) | async-done | bytes 589856 | tf_op jit(solution)/shard_map/gather_texts/all_to_all | solution.py:23
  46.1 6.3 %coefficients.1 = (bf16[256,1152]{1,0:T(8,128)(2,1)}, bf16[256,512]{1,0:T(8,128)(2,1)}, bf16[256,512]{1,0:T(8,128)(2,1)}, bf16[256,2,576]{2,1,0:T(2,128)(2,1)}) custom-call(f32[3]{0:T(128)S(1)} %pad_maximum_fusion.scalars, s32[256,1]{1,0:T(8,128)S(1)} %fusion.3.columns, bf16[256,2,576]{2,1,0:T(2,128)(2,1)S(1)} %all-to-all-done.halves, s32[1,512]{1,0:T(1,128)S(1)} %bitcast.2, ...), custom_call_target="tpu_custom_call" | custom-call | flops 1207959552 | bytes 2359296 | tf_op jit(solution)/shard_map/coefficients/pallas_call | solution.py:188
  52.4 9.8 %all-to-all-start.1 = ((bf16[256,2,576]{2,1,0:T(2,128)(2,1)}), bf16[256,2,576]{2,1,0:T(2,128)(2,1)S(1)}, u32[]{:S(2)}, u32[]{:S(2)}) async-start(bf16[256,2,576]{2,1,0:T(2,128)(2,1)} %get-tuple-element.21), calls=%async_computation.1 | async-start | bytes 1310720 | tf_op jit(solution)/shard_map/text_grad/all_to_all | solution.py:23
  62.2 2.9 %image_grad.2 = (f32[128,1152]{1,0:T(8,128)}, f32[128,1152]{1,0:T(8,128)}, f32[128,1152]{1,0:T(8,128)}, f32[128,1152]{1,0:T(8,128)}) custom-call(bf16[256,512]{1,0:T(8,128)(2,1)} %get-tuple-element.16.coef_in, bf16[256,1152]{1,0:T(8,128)(2,1)} %get-tuple-element.15.block_in), custom_call_target="tpu_custom_call" | custom-call | flops 301989888 | bytes 2359296 | tf_op jit(solution)/shard_map/image_grad/pallas_call | solution.py:224
  65.1 1.9 %collective-permute-start.3 = (f32[128,1152]{1,0:T(8,128)}, f32[128,1152]{1,0:T(8,128)S(1)}, u32[]{:S(2)}, u32[]{:S(2)}) collective-permute-start(f32[128,1152]{1,0:T(8,128)} %get-tuple-element.17), channel_id=1, source_target_pairs={{0,16},{16,0},{1,17},{17,1},{2,18},{18,2},{3,19},{19,3},{4,20},{20... | collective-permute-start | bytes 1769480 | tf_op jit(solution)/shard_map/image_grad/ppermute | solution.py:19
  67.0 2.4 %collective-permute-start.4 = (f32[128,1152]{1,0:T(8,128)}, f32[128,1152]{1,0:T(8,128)S(1)}, u32[]{:S(2)}, u32[]{:S(2)}) collective-permute-start(f32[128,1152]{1,0:T(8,128)} %get-tuple-element.18), channel_id=1, source_target_pairs={{0,16},{16,0},{1,17},{17,1},{2,18},{18,2},{3,19},{19,3},{4,20},{20... | collective-permute-start | bytes 1769480 | tf_op jit(solution)/shard_map/image_grad/ppermute | solution.py:19
  69.5 1.9 %collective-permute-start.5 = (f32[128,1152]{1,0:T(8,128)}, f32[128,1152]{1,0:T(8,128)S(1)}, u32[]{:S(2)}, u32[]{:S(2)}) collective-permute-start(f32[128,1152]{1,0:T(8,128)} %get-tuple-element.19), channel_id=1, source_target_pairs={{0,16},{16,0},{1,17},{17,1},{2,18},{18,2},{3,19},{19,3},{4,20},{20... | collective-permute-start | bytes 1769480 | tf_op jit(solution)/shard_map/image_grad/ppermute | solution.py:19
  71.4 2.4 %collective-permute-start.6 = (f32[128,1152]{1,0:T(8,128)}, f32[128,1152]{1,0:T(8,128)S(1)}, u32[]{:S(2)}, u32[]{:S(2)}) collective-permute-start(f32[128,1152]{1,0:T(8,128)} %get-tuple-element.20), channel_id=1, source_target_pairs={{0,16},{16,0},{1,17},{17,1},{2,18},{18,2},{3,19},{19,3},{4,20},{20... | collective-permute-start | bytes 1769480 | tf_op jit(solution)/shard_map/image_grad/ppermute | solution.py:19
  73.8 0.0 collective-permute-done.3.refs_0_
  73.8 0.0 collective-permute-done.4.refs_1_
  73.8 0.0 collective-permute-done.5.refs_2_
  73.8 1.8 %collective-permute-done.6.refs_3_ = f32[128,1152]{1,0:T(8,128)S(1)} collective-permute-done((f32[128,1152]{1,0:T(8,128)}, f32[128,1152]{1,0:T(8,128)S(1)}, u32[]{:S(2)}, u32[]{:S(2)}) %collective-permute-start.6) | collective-permute-done | bytes 589856 | tf_op jit(solution)/shard_map/image_grad/ppermute | solution.py:19
  75.6 3.2 %image_grad.3 = bf16[512,1152]{1,0:T(8,128)(2,1)} custom-call(bf16[256,512]{1,0:T(8,128)(2,1)} %get-tuple-element.14.coef_in, bf16[256,1152]{1,0:T(8,128)(2,1)} %get-tuple-element.15.block_in, f32[128,1152]{1,0:T(8,128)S(1)} %collective-permute-done.3.refs_0_, f32[128,1152]{1,0:T(8,128)S(1)} %collective-permute-done.4.refs_1_, ...), custom_call_target="tpu_custom_call" | custom-call | flops 301989888 | bytes 3538944 | tf_op jit(solution)/shard_map/image_grad/pallas_call | solution.py:239
  78.8 4.7 %all-to-all-done.1 = bf16[256,2,576]{2,1,0:T(2,128)(2,1)S(1)} async-done(((bf16[256,2,576]{2,1,0:T(2,128)(2,1)}), bf16[256,2,576]{2,1,0:T(2,128)(2,1)S(1)}, u32[]{:S(2)}, u32[]{:S(2)}) %all-to-all-start.1) | async-done | bytes 589856 | tf_op jit(solution)/shard_map/text_grad/all_to_all | solution.py:23
  83.5 0.6 reduce_sum.12
  84.1 0.7 convert_element_type.13
Async XLA Ops:
  0.6 0.7 copy-start
  2.3 28.0 %copy-start.1 = (s32[512]{0:T(512)S(1)}, s32[512]{0:T(512)}, u32[]{:S(2)}) copy-start(s32[512]{0:T(512)} %param.8) | copy-start | bytes 6148
  2.3 43.8 %all-to-all-start = ((bf16[256,2,576]{2,1,0:T(2,128)(2,1)}), bf16[256,2,576]{2,1,0:T(2,128)(2,1)S(1)}, u32[]{:S(2)}, u32[]{:S(2)}) async-start(bf16[256,2,576]{2,1,0:T(2,128)(2,1)} %gather_texts.1), calls=%async_computation | async-start | bytes 1310720 | tf_op jit(solution)/shard_map/gather_texts/all_to_all | solution.py:23
  25.9 8.4 %collective-permute-start.1 = (bf16[256,1152]{1,0:T(8,128)(2,1)}, bf16[256,1152]{1,0:T(8,128)(2,1)S(1)}, u32[]{:S(2)}, u32[]{:S(2)}) collective-permute-start(bf16[256,1152]{1,0:T(8,128)(2,1)} %get-tuple-element.12), channel_id=1, source_target_pairs={{0,16},{16,0},{1,17},{17,1},{2,18},{18,2},{3,19},{19,3},{4,20},{20... | collective-permute-start | bytes 1769480 | tf_op jit(solution)/shard_map/swap_images/ppermute | solution.py:19
  27.9 6.5 %collective-permute-start.2 = (bf16[256,1152]{1,0:T(8,128)(2,1)}, bf16[256,1152]{1,0:T(8,128)(2,1)S(1)}, u32[]{:S(2)}, u32[]{:S(2)}) collective-permute-start(bf16[256,1152]{1,0:T(8,128)(2,1)} %get-tuple-element.13), channel_id=1, source_target_pairs={{0,16},{16,0},{1,17},{17,1},{2,18},{18,2},{3,19},{19,3},{4,20},{20... | collective-permute-start | bytes 1769480 | tf_op jit(solution)/shard_map/swap_images/ppermute | solution.py:19
  30.3 4.1 %collective-permute-start = (s32[512]{0:T(512)S(1)}, s32[512]{0:T(512)S(1)}, u32[]{:S(2)}, u32[]{:S(2)}) collective-permute-start(s32[512]{0:T(512)S(1)} %copy-done.1), channel_id=1, source_target_pairs={{0,16},{16,0},{1,17},{17,1},{2,18},{18,2},{3,19},{19,3},{4,20},{20... | collective-permute-start | bytes 6152 | tf_op jit(solution)/shard_map/swap_images/ppermute | solution.py:19
  52.4 31.1 %all-to-all-start.1 = ((bf16[256,2,576]{2,1,0:T(2,128)(2,1)}), bf16[256,2,576]{2,1,0:T(2,128)(2,1)S(1)}, u32[]{:S(2)}, u32[]{:S(2)}) async-start(bf16[256,2,576]{2,1,0:T(2,128)(2,1)} %get-tuple-element.21), calls=%async_computation.1 | async-start | bytes 1310720 | tf_op jit(solution)/shard_map/text_grad/all_to_all | solution.py:23
  65.1 8.7 %collective-permute-start.3 = (f32[128,1152]{1,0:T(8,128)}, f32[128,1152]{1,0:T(8,128)S(1)}, u32[]{:S(2)}, u32[]{:S(2)}) collective-permute-start(f32[128,1152]{1,0:T(8,128)} %get-tuple-element.17), channel_id=1, source_target_pairs={{0,16},{16,0},{1,17},{17,1},{2,18},{18,2},{3,19},{19,3},{4,20},{20... | collective-permute-start | bytes 1769480 | tf_op jit(solution)/shard_map/image_grad/ppermute | solution.py:19
  67.0 6.8 %collective-permute-start.4 = (f32[128,1152]{1,0:T(8,128)}, f32[128,1152]{1,0:T(8,128)S(1)}, u32[]{:S(2)}, u32[]{:S(2)}) collective-permute-start(f32[128,1152]{1,0:T(8,128)} %get-tuple-element.18), channel_id=1, source_target_pairs={{0,16},{16,0},{1,17},{17,1},{2,18},{18,2},{3,19},{19,3},{4,20},{20... | collective-permute-start | bytes 1769480 | tf_op jit(solution)/shard_map/image_grad/ppermute | solution.py:19
  69.5 4.4 %collective-permute-start.5 = (f32[128,1152]{1,0:T(8,128)}, f32[128,1152]{1,0:T(8,128)S(1)}, u32[]{:S(2)}, u32[]{:S(2)}) collective-permute-start(f32[128,1152]{1,0:T(8,128)} %get-tuple-element.19), channel_id=1, source_target_pairs={{0,16},{16,0},{1,17},{17,1},{2,18},{18,2},{3,19},{19,3},{4,20},{20... | collective-permute-start | bytes 1769480 | tf_op jit(solution)/shard_map/image_grad/ppermute | solution.py:19
  71.4 4.2 %collective-permute-start.6 = (f32[128,1152]{1,0:T(8,128)}, f32[128,1152]{1,0:T(8,128)S(1)}, u32[]{:S(2)}, u32[]{:S(2)}) collective-permute-start(f32[128,1152]{1,0:T(8,128)} %get-tuple-element.20), channel_id=1, source_target_pairs={{0,16},{16,0},{1,17},{17,1},{2,18},{18,2},{3,19},{19,3},{4,20},{20... | collective-permute-start | bytes 1769480 | tf_op jit(solution)/shard_map/image_grad/ppermute | solution.py:19

commit v3 on v1

v3 whole, which is shorter than its diff:
```python
import jax
import jax.numpy as jnp
from jax import lax
from jax.experimental import pallas as pl
from jax.experimental.pallas import tpu as pltpu
from jax.sharding import Mesh
from jax.sharding import PartitionSpec as P

WIDE = ("far", "zl")
IN_PIECES = 2
OUT_PIECES = 4
HBM = pl.BlockSpec(memory_space=pltpu.HBM)
VMEM = pl.BlockSpec(memory_space=pltpu.VMEM)
SMEM = pl.BlockSpec(memory_space=pltpu.SMEM)
PARAMS = pltpu.CompilerParams(vmem_limit_bytes=24 << 20)


def swap_cores(*arrays):
    return [lax.ppermute(array, "core", [(0, 1), (1, 0)]) for array in arrays]


def exchange(array, axes):
    return lax.all_to_all(array, axes, 0, 0, tiled=True)


def dot(left, right, along):
    return lax.dot_general(
        left, right, ((along[:1], along[1:]), ((), ())), preferred_element_type=jnp.float32
    )


def put(space, *arrays):
    return [pltpu.with_memory_space_constraint(array, space) for array in arrays]


def cost(flops, moved, exps=0):
    return pl.CostEstimate(flops=flops, bytes_accessed=moved, transcendentals=exps)


def repeat_kernel(row, out):
    width = out.shape[2]
    values = row[...].astype(jnp.float32)
    halves = jnp.concatenate([values[:, :width], values[:, width:]], 0).astype(out.dtype)
    out[...] = jnp.broadcast_to(halves[None], out.shape)


def spread_kernel(halves, out):
    rows = halves[...].reshape(out.shape[1:])
    for index in range(out.shape[0]):
        out[index] = rows


def gather_kernel(blocks, out):
    total = blocks[0].astype(jnp.float32)
    for index in range(1, blocks.shape[0]):
        total = total + blocks[index].astype(jnp.float32)
    width = out.shape[2]
    out[:, 0, :] = total[:, :width].astype(out.dtype)
    out[:, 1, :] = total[:, width:].astype(out.dtype)


def sum_kernel(parts, out):
    total = jnp.sum(parts[...].astype(jnp.float32), axis=0)
    width = parts.shape[2]
    out[:, :width] = total[0:1].astype(out.dtype)
    out[:, width:] = total[1:2].astype(out.dtype)


def split_kernel(whole, *refs):
    *pieces, held, sems, out_sems = refs
    size = pieces[0].shape[0]
    loads, stores = [], []
    for index, piece in enumerate(pieces):
        span = pl.ds(index * size, size)
        loads.append(pltpu.make_async_copy(whole.at[span], held.at[index], sems.at[index]))
        stores.append(pltpu.make_async_copy(held.at[index], piece, out_sems.at[index]))
    for load in loads:
        load.start()
    for load, store in zip(loads, stores):
        load.wait()
        store.start()
    for store in stores:
        store.wait()


def coefficients(block, frames, paired, columns, scalars):
    factor, offset, weight = scalars[0], scalars[1], scalars[2]
    logits = factor * dot(block, frames, (1, 1)) + offset
    own = paired == columns
    value = jax.nn.sigmoid(jnp.where(own, -logits, logits)) * jnp.where(own, -weight, weight)
    return value.astype(jnp.bfloat16)


def text_kernel(scalars, columns, texts, labels, other_labels, images, *refs):
    *others, coef, part = refs
    block = texts[...].reshape(part.shape)
    value = coefficients(block, images[...], labels[...], columns[...], scalars)
    coef[...] = value
    terms = [(value, images)]
    for index, frames in enumerate(others):
        size = frames.shape[0]
        paired = other_labels[:, pl.ds(index * size, size)]
        terms.append((coefficients(block, frames[...], paired, columns[...], scalars), frames))
    total = sum(dot(value, frames[...], (1, 0)) for value, frames in terms)
    part[...] = total.astype(part.dtype)


def image_kernel(scalars, columns, labels, coef, texts, other_texts, images, out, *scratch):
    result, out_sems = scratch
    block = texts[...].reshape(-1, texts.shape[2])
    other = other_texts[...].reshape(-1, texts.shape[2])
    value = coefficients(other, images[...], labels[...], columns[...], scalars)
    size = result.shape[1]
    stores = []
    for index in range(result.shape[0]):
        span = slice(index * size, (index + 1) * size)
        total = dot(coef[:, span], block, (0, 0)) + dot(value[:, span], other, (0, 0))
        result[index] = total.astype(result.dtype)
        target = out.at[pl.ds(index * size, size)]
        stores.append(pltpu.make_async_copy(result.at[index], target, out_sems.at[index]))
        stores[-1].start()
    for store in stores:
        store.wait()


def local(images, texts, labels, log_scale, bias, loss_scale):
    far, cores, x, zl = (lax.axis_size(name) for name in ("far", "core", "x", "zl"))
    core = lax.axis_index("core")
    rows = images.shape[0]
    width = texts.shape[1]
    shared = far * x * zl
    factor = jnp.exp(log_scale[0])
    weight = factor * loss_scale[0] / (rows * shared * cores)
    scalars = jnp.stack([factor, bias[0], weight])
    flops = 2 * shared * rows * width

    place = jnp.arange(shared, dtype=jnp.int32)
    first = place // zl % far * (cores * x * zl) + place // (far * zl) * zl + place % zl
    columns = (first + core * x * zl)[:, None]
    columns_other = (first + (1 - core) * x * zl)[:, None]
    half = width // 2
    plane = far * zl

    with jax.named_scope("gather_texts"):
        halves = pl.pallas_call(
            repeat_kernel,
            out_shape=jax.ShapeDtypeStruct((plane, 2, half), texts.dtype),
            in_specs=[VMEM],
            out_specs=VMEM,
            compiler_params=PARAMS,
        )(texts)
        halves = exchange(halves, WIDE)
        blocks = pl.pallas_call(
            spread_kernel,
            out_shape=jax.ShapeDtypeStruct((x, plane, width), texts.dtype),
            in_specs=[VMEM],
            out_specs=VMEM,
            compiler_params=PARAMS,
        )(halves)
        blocks = exchange(blocks, "x")

    with jax.named_scope("swap_images"):
        pieces = pl.pallas_call(
            split_kernel,
            out_shape=[pltpu.HBM((rows // IN_PIECES, width), images.dtype)] * IN_PIECES,
            in_specs=[HBM],
            out_specs=[HBM] * IN_PIECES,
            scratch_shapes=[
                pltpu.VMEM((IN_PIECES, rows // IN_PIECES, width), images.dtype),
                pltpu.SemaphoreType.DMA((IN_PIECES,)),
                pltpu.SemaphoreType.DMA((IN_PIECES,)),
            ],
            compiler_params=PARAMS,
            cost_estimate=cost(0, 4 * rows * width),
        )(*put(pltpu.HBM, images))
        *others, labels_other = swap_cores(*pieces, labels)

    with jax.named_scope("coefficients"):
        coef, part = pl.pallas_call(
            text_kernel,
            out_shape=(
                jax.ShapeDtypeStruct((shared, rows), jnp.bfloat16),
                jax.ShapeDtypeStruct((shared, width), jnp.bfloat16),
            ),
            in_specs=[SMEM] + [VMEM] * (5 + IN_PIECES),
            out_specs=(VMEM, VMEM),
            compiler_params=PARAMS,
            cost_estimate=cost(4 * flops, 4 * rows * width, 2 * shared * rows),
        )(
            scalars,
            columns,
            *put(pltpu.VMEM, blocks),
            labels[None, :],
            labels_other[None, :],
            *put(pltpu.VMEM, images, *others),
        )

    with jax.named_scope("text_grad"):
        blocks_grad = exchange(part.reshape(x, plane, width), "x")
        summed = pl.pallas_call(
            gather_kernel,
            out_shape=jax.ShapeDtypeStruct((plane, 2, half), jnp.bfloat16),
            in_specs=[VMEM],
            out_specs=VMEM,
            compiler_params=PARAMS,
        )(blocks_grad)
        text_grad = pl.pallas_call(
            sum_kernel,
            out_shape=jax.ShapeDtypeStruct((1, width), jnp.bfloat16),
            in_specs=[VMEM],
            out_specs=VMEM,
            compiler_params=PARAMS,
        )(exchange(summed, WIDE))

    with jax.named_scope("image_grad"):
        (blocks_other,) = swap_cores(blocks)
        image_grad = pl.pallas_call(
            image_kernel,
            out_shape=jax.ShapeDtypeStruct((rows, width), jnp.bfloat16),
            in_specs=[SMEM] + [VMEM] * 6,
            out_specs=HBM,
            scratch_shapes=[
                pltpu.VMEM((OUT_PIECES, rows // OUT_PIECES, width), jnp.bfloat16),
                pltpu.SemaphoreType.DMA((OUT_PIECES,)),
            ],
            compiler_params=PARAMS,
            cost_estimate=cost(3 * flops, 6 * rows * width, shared * rows),
        )(
            scalars,
            columns_other,
            labels[None, :],
            coef,
            blocks,
            blocks_other,
            images,
        )
    return (image_grad, text_grad)


def solution(mesh):
    blk, grp = mesh.devices.shape
    rows = ("far", "core", "x", "zl")
    fine = Mesh(mesh.devices.reshape(blk // 2, 2, 4, grp // 4), rows)
    placed = (P(rows, None), P(rows, None), P(rows), P(), P(), P())
    return jax.shard_map(
        local,
        mesh=fine,
        in_specs=placed,
        out_specs=(P(rows, None), P(rows, None)),
        check_vma=False,
    )
```

time: 102 us -> 84.4 us (0.83); the launches traced: 102 us -> 83.1 us
  blocking collectives: 44.9 us -> 0 us
  starting transfers between devices: 13 us -> 44.3 us
  Pallas kernels: 0 us -> 11.9 us
  other arithmetic: 7.13 us -> 0.18 us
  local copies, waits for them, and re-layouts: 6.71 us -> 0.69 us
  matrix products: 4.28 us -> 0 us
    all_to_all x1 -> x0, blocking collectives: 44.9 us -> none  [exchange(): return lax.all_to_all(array, WIDE, 0, 0, tiled=True)]
    all_to_all x1 -> x4, starting transfers between devices: 8.51 us -> 36 us  [exchange(): return lax.all_to_all(array, axes, 0, 0, tiled=True)]
    pallas_call x0 -> x7, Pallas kernels: none -> 11.9 us  [the longest x1 3.64 us: local(): pl.pallas_call(text_kernel, out_shape=(jax.ShapeDtypeStruct((shared, rows...]
    unnamed x17 -> x6, local copies, waits for them, and re-layouts: 4.99 us -> 0.69 us
    dot_general x5 -> x0, matrix products: 4.28 us -> none  [the longest x1 1.89 us: local(): jnp.dot(jnp.concatenate([coef_mine, coef_other], 1), jnp.concatenate([min...]
    broadcast_in_dim x1 -> x0, other arithmetic: 4.21 us -> none  [local(): mine = exchange(jnp.broadcast_to(texts, (shared, texts.shape[1])))]
    ppermute x2 -> x4, starting transfers between devices: 4.5 us -> 8.28 us  [swap_cores(): return [lax.ppermute(array, 'core', [(0, 1), (1, 0)]) for array in arrays]]
    broadcast_in_dim x2 -> x0, local copies, waits for them, and re-layouts: 1.13 us -> none  [local(): mine = exchange(jnp.broadcast_to(texts, (shared, texts.shape[1])))]
  transfers between devices with their start and end apart: 3 -> 8, of which waited for: 2 -> 4; matrix products, arithmetic and copies ran while one was open for 3% -> 0% of each run, Pallas kernels for 0% -> 8%
where the time goes in v3:
time: 84.4 us; the launch traced here: 83.1 us
  starting transfers between devices  44.3 us (52%)
  waiting for transfers between devices  23.3 us (28%)
  Pallas kernels  11.9 us (14%)
  between operations  2.75 us (3%)
    all_to_all x4, starting transfers between devices, exchange(): return lax.all_to_all(array, axes, 0, 0, tiled=True)  36 us
    all_to_all x4, waiting for transfers between devices, exchange(): return lax.all_to_all(array, axes, 0, 0, tiled=True)  23.3 us
    ppermute x4, starting transfers between devices, swap_cores(): return [lax.ppermute(array, 'core', [(0, 1), (1, 0)]) for array in arrays]  8.28 us
    pallas_call x1, Pallas kernels, local(): pl.pallas_call(text_kernel, out_shape=(jax.ShapeDtypeStruct((shared, rows...  3.64 us
    pallas_call x1, Pallas kernels, local(): pl.pallas_call(image_kernel, out_shape=jax.ShapeDtypeStruct((rows, width)...  2.76 us
    pallas_call x1, Pallas kernels, local(): pl.pallas_call(split_kernel, out_shape=[pltpu.HBM((rows // IN_PIECES, wid...  2.13 us
  transfers between devices with their start and end apart: 8, of which 4 were waited for; matrix products, arithmetic and copies ran while one was open for 0% of the time, Pallas kernels for 8%

profile of v3, /device:TPU:6, one launch (start us, length us, event | category | flops | bytes accessed | tf_op | source)
XLA Modules:
  0.0 83.1 jit_solution(11423853614655107802)
XLA Ops:
  0.6 0.0 copy-start.1
  0.6 0.7 copy-done.1
  1.3 0.8 gather_texts.2
  2.1 16.6 %all-to-all-start = ((bf16[64,2,576]{2,1,0:T(2,128)(2,1)}), bf16[64,2,576]{2,1,0:T(2,128)(2,1)S(1)}, u32[]{:S(2)}, u32[]{:S(2)}) async-start(bf16[64,2,576]{2,1,0:T(2,128)(2,1)} %gather_texts.2), calls=%async_computation | async-start | bytes 327680 | tf_op jit(solution)/shard_map/gather_texts/all_to_all | solution.py:23
  18.7 2.1 %swap_images.1 = (bf16[256,1152]{1,0:T(8,128)(2,1)}, bf16[256,1152]{1,0:T(8,128)(2,1)}) custom-call(bf16[512,1152]{1,0:T(8,128)(2,1)} %images.3), custom_call_target="tpu_custom_call" | custom-call | bytes 2359296 | tf_op jit(solution)/shard_map/swap_images/pallas_call | solution.py:163
  20.8 0.0 copy-start.2
  20.8 0.0 copy-start
  20.8 2.1 %collective-permute-start.1 = (bf16[256,1152]{1,0:T(8,128)(2,1)}, bf16[256,1152]{1,0:T(8,128)(2,1)S(1)}, u32[]{:S(2)}, u32[]{:S(2)}) collective-permute-start(bf16[256,1152]{1,0:T(8,128)(2,1)} %get-tuple-element.6), channel_id=1, source_target_pairs={{0,16},{16,0},{1,17},{17,1},{2,18},{18,2},{3,19},{19,3},{4,20},{20... | collective-permute-start | bytes 1769480 | tf_op jit(solution)/shard_map/swap_images/ppermute | solution.py:19
  22.9 2.4 %collective-permute-start.2 = (bf16[256,1152]{1,0:T(8,128)(2,1)}, bf16[256,1152]{1,0:T(8,128)(2,1)}, u32[]{:S(2)}, u32[]{:S(2)}) collective-permute-start(bf16[256,1152]{1,0:T(8,128)(2,1)} %get-tuple-element.7), channel_id=1, source_target_pairs={{0,16},{16,0},{1,17},{17,1},{2,18},{18,2},{3,19},{19,3},{4,20},{20... | collective-permute-start | bytes 1769480 | tf_op jit(solution)/shard_map/swap_images/ppermute | solution.py:19
  25.3 6.6 %all-to-all-done.halves = bf16[64,2,576]{2,1,0:T(2,128)(2,1)S(1)} async-done(((bf16[64,2,576]{2,1,0:T(2,128)(2,1)}), bf16[64,2,576]{2,1,0:T(2,128)(2,1)S(1)}, u32[]{:S(2)}, u32[]{:S(2)}) %all-to-all-start) | async-done | bytes 147488 | tf_op jit(solution)/shard_map/gather_texts/all_to_all | solution.py:23
  31.9 0.9 %gather_texts.3 = bf16[4,64,1152]{2,1,0:T(8,128)(2,1)} custom-call(bf16[64,2,576]{2,1,0:T(2,128)(2,1)S(1)} %all-to-all-done.halves), custom_call_target="tpu_custom_call" | custom-call | tf_op jit(solution)/shard_map/gather_texts/pallas_call | solution.py:153
  32.8 4.8 %all-to-all-start.1 = ((bf16[4,64,1152]{2,1,0:T(8,128)(2,1)}), bf16[4,64,1152]{2,1,0:T(8,128)(2,1)S(1)}, u32[]{:S(2)}, u32[]{:S(2)}) async-start(bf16[4,64,1152]{2,1,0:T(8,128)(2,1)} %gather_texts.3), calls=%async_computation.1 | async-start | bytes 1179648 | tf_op jit(solution)/shard_map/gather_texts/all_to_all | solution.py:23
  37.6 0.0 copy-done.2
  37.6 1.9 %collective-permute-start = (s32[512]{0:T(512)S(1)}, s32[512]{0:T(512)S(1)}, u32[]{:S(2)}, u32[]{:S(2)}) collective-permute-start(s32[512]{0:T(512)S(1)} %copy-done.2), channel_id=1, source_target_pairs={{0,16},{16,0},{1,17},{17,1},{2,18},{18,2},{3,19},{19,3},{4,20},{20... | collective-permute-start | bytes 6152 | tf_op jit(solution)/shard_map/swap_images/ppermute | solution.py:19
  41.5 0.1 broadcast_add_fusion.columns
  41.6 0.1 pad_maximum_fusion.scalars
  41.6 0.0 collective-permute-done
  41.6 0.0 collective-permute-done.1.refs_0_
  41.6 0.0 collective-permute-done.2.refs_1_
  41.6 2.3 %all-to-all-done.1.texts = bf16[4,64,1152]{2,1,0:T(8,128)(2,1)S(1)} async-done(((bf16[4,64,1152]{2,1,0:T(8,128)(2,1)}), bf16[4,64,1152]{2,1,0:T(8,128)(2,1)S(1)}, u32[]{:S(2)}, u32[]{:S(2)}) %all-to-all-start.1) | async-done | bytes 589856 | tf_op jit(solution)/shard_map/gather_texts/all_to_all | solution.py:23
  44.0 0.0 copy-done
  44.0 3.6 %coefficients.1 = (bf16[256,512]{1,0:T(8,128)(2,1)S(1)}, bf16[256,1152]{1,0:T(8,128)(2,1)}) custom-call(f32[3]{0:T(128)S(1)} %pad_maximum_fusion.scalars, s32[256,1]{1,0:T(8,128)S(1)} %broadcast_add_fusion.columns, bf16[4,64,1152]{2,1,0:T(8,128)(2,1)S(1)} %all-to-all-done.1.texts, s32[1,512]{1,0:T(1,128)S(1)} %bitcast.3, s32[1,512]{1,0:T(1,128)S(1)} %bitcast.5, ...), custom_call_target="tpu_custom_call" | custom-call | flops 1207959552 | bytes 2359296 | tf_op jit(solution)/shard_map/coefficients/pallas_call | solution.py:179
  47.6 5.5 %all-to-all-start.2 = ((bf16[4,64,1152]{2,1,0:T(8,128)(2,1)}), bf16[4,64,1152]{2,1,0:T(8,128)(2,1)S(1)}, u32[]{:S(2)}, u32[]{:S(2)}) async-start(bf16[4,64,1152]{2,1,0:T(8,128)(2,1)} %bitcast.2), calls=%async_computation.2 | async-start | bytes 1179648 | tf_op jit(solution)/shard_map/text_grad/all_to_all | solution.py:23
  53.1 1.9 %collective-permute-start.3 = (bf16[4,64,1152]{2,1,0:T(8,128)(2,1)S(1)}, bf16[4,64,1152]{2,1,0:T(8,128)(2,1)S(1)}, u32[]{:S(2)}, u32[]{:S(2)}) collective-permute-start(bf16[4,64,1152]{2,1,0:T(8,128)(2,1)S(1)} %all-to-all-done.1.texts), channel_id=1, source_target_pairs={{0,16},{16,0},{1,17},{17,1},{2,18},{18,2},{3,19},{19,3},{4,20},{20... | collective-permute-start | bytes 1769480 | tf_op jit(solution)/shard_map/image_grad/ppermute | solution.py:19
  55.0 4.4 %all-to-all-done.2.blocks = bf16[4,64,1152]{2,1,0:T(8,128)(2,1)S(1)} async-done(((bf16[4,64,1152]{2,1,0:T(8,128)(2,1)}), bf16[4,64,1152]{2,1,0:T(8,128)(2,1)S(1)}, u32[]{:S(2)}, u32[]{:S(2)}) %all-to-all-start.2) | async-done | bytes 589856 | tf_op jit(solution)/shard_map/text_grad/all_to_all | solution.py:23
  59.5 0.9 %text_grad.2 = bf16[64,2,576]{2,1,0:T(2,128)(2,1)} custom-call(bf16[4,64,1152]{2,1,0:T(8,128)(2,1)S(1)} %all-to-all-done.2.blocks), custom_call_target="tpu_custom_call" | custom-call | tf_op jit(solution)/shard_map/text_grad/pallas_call | solution.py:200
  60.3 9.1 %all-to-all-start.3 = ((bf16[64,2,576]{2,1,0:T(2,128)(2,1)}), bf16[64,2,576]{2,1,0:T(2,128)(2,1)S(1)}, u32[]{:S(2)}, u32[]{:S(2)}) async-start(bf16[64,2,576]{2,1,0:T(2,128)(2,1)} %text_grad.2), calls=%async_computation.3 | async-start | bytes 327680 | tf_op jit(solution)/shard_map/text_grad/all_to_all | solution.py:23
  69.5 0.1 broadcast_add_fusion.1.columns
  69.5 0.0 collective-permute-done.3.other_texts
  69.5 2.8 %image_grad.1 = bf16[512,1152]{1,0:T(8,128)(2,1)} custom-call(f32[3]{0:T(128)S(1)} %pad_maximum_fusion.scalars, s32[256,1]{1,0:T(8,128)S(1)} %broadcast_add_fusion.1.columns, s32[1,512]{1,0:T(1,128)S(1)} %bitcast.4, bf16[256,512]{1,0:T(8,128)(2,1)S(1)} %get-tuple-element.8.coef, bf16[4,64,1152]{2,1,0:T(8,128)(2,1)S(1)} %all-to-all-done.1.texts, ...), custom_call_target="tpu_custom_call" | custom-call | flops 905969664 | bytes 3538944 | tf_op jit(solution)/shard_map/image_grad/pallas_call | solution.py:217
  72.3 10.0 %all-to-all-done.3.parts = bf16[64,2,576]{2,1,0:T(2,128)(2,1)S(1)} async-done(((bf16[64,2,576]{2,1,0:T(2,128)(2,1)}), bf16[64,2,576]{2,1,0:T(2,128)(2,1)S(1)}, u32[]{:S(2)}, u32[]{:S(2)}) %all-to-all-start.3) | async-done | bytes 147488 | tf_op jit(solution)/shard_map/text_grad/all_to_all | solution.py:23
  82.3 0.8 %text_grad.3 = bf16[1,1152]{1,0:T(2,128)(2,1)} custom-call(bf16[64,2,576]{2,1,0:T(2,128)(2,1)S(1)} %all-to-all-done.3.parts), custom_call_target="tpu_custom_call" | custom-call | tf_op jit(solution)/shard_map/text_grad/pallas_call | solution.py:207
Async XLA Ops:
  0.6 0.7 copy-start.1
  2.1 29.8 %all-to-all-start = ((bf16[64,2,576]{2,1,0:T(2,128)(2,1)}), bf16[64,2,576]{2,1,0:T(2,128)(2,1)S(1)}, u32[]{:S(2)}, u32[]{:S(2)}) async-start(bf16[64,2,576]{2,1,0:T(2,128)(2,1)} %gather_texts.2), calls=%async_computation | async-start | bytes 327680 | tf_op jit(solution)/shard_map/gather_texts/all_to_all | solution.py:23
  20.8 16.8 %copy-start.2 = (s32[512]{0:T(512)S(1)}, s32[512]{0:T(512)}, u32[]{:S(2)}) copy-start(s32[512]{0:T(512)} %param.8) | copy-start | bytes 6148
  20.8 23.1 %copy-start = (bf16[512,1152]{1,0:T(8,128)(2,1)S(1)}, bf16[512,1152]{1,0:T(8,128)(2,1)}, u32[]{:S(2)}) copy-start(bf16[512,1152]{1,0:T(8,128)(2,1)} %images.3) | copy-start | bytes 3538948
  20.8 20.8 %collective-permute-start.1 = (bf16[256,1152]{1,0:T(8,128)(2,1)}, bf16[256,1152]{1,0:T(8,128)(2,1)S(1)}, u32[]{:S(2)}, u32[]{:S(2)}) collective-permute-start(bf16[256,1152]{1,0:T(8,128)(2,1)} %get-tuple-element.6), channel_id=1, source_target_pairs={{0,16},{16,0},{1,17},{17,1},{2,18},{18,2},{3,19},{19,3},{4,20},{20... | collective-permute-start | bytes 1769480 | tf_op jit(solution)/shard_map/swap_images/ppermute | solution.py:19
  22.9 18.7 %collective-permute-start.2 = (bf16[256,1152]{1,0:T(8,128)(2,1)}, bf16[256,1152]{1,0:T(8,128)(2,1)}, u32[]{:S(2)}, u32[]{:S(2)}) collective-permute-start(bf16[256,1152]{1,0:T(8,128)(2,1)} %get-tuple-element.7), channel_id=1, source_target_pairs={{0,16},{16,0},{1,17},{17,1},{2,18},{18,2},{3,19},{19,3},{4,20},{20... | collective-permute-start | bytes 1769480 | tf_op jit(solution)/shard_map/swap_images/ppermute | solution.py:19
  32.8 11.1 %all-to-all-start.1 = ((bf16[4,64,1152]{2,1,0:T(8,128)(2,1)}), bf16[4,64,1152]{2,1,0:T(8,128)(2,1)S(1)}, u32[]{:S(2)}, u32[]{:S(2)}) async-start(bf16[4,64,1152]{2,1,0:T(8,128)(2,1)} %gather_texts.3), calls=%async_computation.1 | async-start | bytes 1179648 | tf_op jit(solution)/shard_map/gather_texts/all_to_all | solution.py:23
  37.6 4.0 %collective-permute-start = (s32[512]{0:T(512)S(1)}, s32[512]{0:T(512)S(1)}, u32[]{:S(2)}, u32[]{:S(2)}) collective-permute-start(s32[512]{0:T(512)S(1)} %copy-done.2), channel_id=1, source_target_pairs={{0,16},{16,0},{1,17},{17,1},{2,18},{18,2},{3,19},{19,3},{4,20},{20... | collective-permute-start | bytes 6152 | tf_op jit(solution)/shard_map/swap_images/ppermute | solution.py:19
  47.6 11.9 %all-to-all-start.2 = ((bf16[4,64,1152]{2,1,0:T(8,128)(2,1)}), bf16[4,64,1152]{2,1,0:T(8,128)(2,1)S(1)}, u32[]{:S(2)}, u32[]{:S(2)}) async-start(bf16[4,64,1152]{2,1,0:T(8,128)(2,1)} %bitcast.2), calls=%async_computation.2 | async-start | bytes 1179648 | tf_op jit(solution)/shard_map/text_grad/all_to_all | solution.py:23
  53.1 16.4 %collective-permute-start.3 = (bf16[4,64,1152]{2,1,0:T(8,128)(2,1)S(1)}, bf16[4,64,1152]{2,1,0:T(8,128)(2,1)S(1)}, u32[]{:S(2)}, u32[]{:S(2)}) collective-permute-start(bf16[4,64,1152]{2,1,0:T(8,128)(2,1)S(1)} %all-to-all-done.1.texts), channel_id=1, source_target_pairs={{0,16},{16,0},{1,17},{17,1},{2,18},{18,2},{3,19},{19,3},{4,20},{20... | collective-permute-start | bytes 1769480 | tf_op jit(solution)/shard_map/image_grad/ppermute | solution.py:19
  60.3 21.9 %all-to-all-start.3 = ((bf16[64,2,576]{2,1,0:T(2,128)(2,1)}), bf16[64,2,576]{2,1,0:T(2,128)(2,1)S(1)}, u32[]{:S(2)}, u32[]{:S(2)}) async-start(bf16[64,2,576]{2,1,0:T(2,128)(2,1)} %text_grad.2), calls=%async_computation.3 | async-start | bytes 327680 | tf_op jit(solution)/shard_map/text_grad/all_to_all | solution.py:23

commit v4 on v3

v4 whole, which is shorter than its diff:
```python
import functools

import jax
import jax.numpy as jnp
from jax import lax
from jax.experimental import pallas as pl
from jax.experimental.pallas import tpu as pltpu
from jax.sharding import Mesh
from jax.sharding import PartitionSpec as P

WIDE = ("far", "zl")
IN_PIECES = 2
OUT_PIECES = 2
TEXT_PIECES = 2
TAIL = 16
HOLD = 1 << 34
HBM = pl.BlockSpec(memory_space=pltpu.HBM)
ANY = pl.BlockSpec(memory_space=pl.ANY)
SMEM = pl.BlockSpec(memory_space=pltpu.SMEM)
VMEM = pl.BlockSpec(memory_space=pltpu.VMEM)
PARAMS = pltpu.CompilerParams(vmem_limit_bytes=24 << 20)


def swap_cores(*arrays):
    return [lax.ppermute(array, "core", [(0, 1), (1, 0)]) for array in arrays]


def exchange(array, axes):
    return lax.all_to_all(array, axes, 0, 0, tiled=True)


def dot(left, right, along):
    return lax.dot_general(
        left, right, ((along[:1], along[1:]), ((), ())), preferred_element_type=jnp.float32
    )


def put(space, *arrays):
    return [pltpu.with_memory_space_constraint(array, space) for array in arrays]


def cost(flops, moved, exps=0):
    return pl.CostEstimate(flops=flops, bytes_accessed=moved, transcendentals=exps)


def repeat_kernel(row, out):
    width = out.shape[2]
    values = row[...].astype(jnp.float32)
    halves = jnp.concatenate([values[:, :width], values[:, width:]], 0).astype(out.dtype)
    out[...] = jnp.broadcast_to(halves[None], out.shape)


def spread_kernel(halves, out):
    rows = halves[...].reshape(out.shape[1:])
    for index in range(out.shape[0]):
        out[index] = rows


def gather_kernel(blocks, after, out):
    del after
    total = blocks[0].astype(jnp.float32)
    for index in range(1, blocks.shape[0]):
        total = total + blocks[index].astype(jnp.float32)
    width = out.shape[2]
    out[:, 0, :] = total[:, :width].astype(out.dtype)
    out[:, 1, :] = total[:, width:].astype(out.dtype)


def sum_kernel(parts, out):
    total = jnp.sum(parts[...].astype(jnp.float32), axis=0)
    width = parts.shape[2]
    out[:, :width] = total[0:1].astype(out.dtype)
    out[:, width:] = total[1:2].astype(out.dtype)


def hold_kernel(array, out):
    del array, out


def hold(array):
    return pl.pallas_call(
        hold_kernel,
        out_shape=jax.ShapeDtypeStruct(array.shape, array.dtype),
        in_specs=[ANY],
        out_specs=ANY,
        input_output_aliases={0: 0},
        compiler_params=PARAMS,
        cost_estimate=cost(HOLD, 0),
    )(array)


def split_kernel(log_scale, bias, loss_scale, whole, labels, after, *refs, frames):
    del after
    *pieces, rows, tails, sems, tail_sems = refs
    size = pieces[0].shape[0] - TAIL
    stores = []
    for index, piece in enumerate(pieces):
        source = whole.at[pl.ds(index * size, size)]
        target = piece.at[pl.ds(0, size)]
        stores.append(pltpu.make_async_copy(source, target, sems.at[index]))
        stores[-1].start()
    line = lax.broadcasted_iota(jnp.int32, (TAIL, size), 0)
    for index, piece in enumerate(pieces):
        label = labels[:, index * size : (index + 1) * size]
        tail = jnp.where(line == 0, label >> 5, jnp.where(line == 1, label & 31, 0))
        tails[index] = jnp.zeros(tails.shape[1:], tails.dtype)
        tails[index, :, :size] = tail.astype(jnp.float32).astype(tails.dtype)
        target = piece.at[pl.ds(size, TAIL)]
        stores.append(pltpu.make_async_copy(tails.at[index], target, tail_sems.at[index]))
        stores[-1].start()
    factor = jnp.exp(jnp.full((1, rows.shape[1]), log_scale[0]))
    rows[0:1, :] = factor
    rows[1:2, :] = jnp.full(factor.shape, bias[0])
    rows[2:3, :] = factor * loss_scale[0] / frames
    for store in stores:
        store.wait()


def coefficients(block, frames, paired, columns, scalars):
    factor, offset, weight = scalars
    logits = factor * dot(block, frames, (1, 1)) + offset
    own = paired == columns
    value = jax.nn.sigmoid(jnp.where(own, -logits, logits)) * jnp.where(own, -weight, weight)
    return value.astype(jnp.bfloat16)


def scales(rows):
    return rows[0:1, 0:1], rows[1:2, 0:1], rows[2:3, 0:1]


def text_kernel(rows, columns, texts, labels, images, *refs):
    others, (coef, part, *copies, held, load_sem, sems) = refs[:IN_PIECES], refs[IN_PIECES:]
    load = pltpu.make_async_copy(images, held, load_sem)
    load.start()
    stores = []
    for index, copy in enumerate(copies):
        source = texts.at[pl.ds(index * copy.shape[0], copy.shape[0])]
        stores.append(pltpu.make_async_copy(source, copy, sems.at[index]))
        stores[-1].start()
    scalars = scales(rows)
    block = texts[...].reshape(part.shape)
    terms = []
    for piece in others:
        size = piece.shape[0] - TAIL
        frames = piece[:size, :]
        tail = piece[size:, :size].astype(jnp.float32)
        paired = (tail[0:1] * 32 + tail[1:2]).astype(jnp.int32)
        terms.append((coefficients(block, frames, paired, columns[...], scalars), frames))
    load.wait()
    value = coefficients(block, held[...], labels[...], columns[...], scalars)
    coef[...] = value
    terms.append((value, held[...]))
    total = sum(dot(value, frames, (1, 0)) for value, frames in terms)
    part[...] = total.astype(part.dtype)
    for store in stores:
        store.wait()


def image_kernel(rows, columns, labels, coef, texts, images, *refs):
    others, (out, done, result, out_sems) = refs[:TEXT_PIECES], refs[TEXT_PIECES:]
    done[...] = jnp.zeros_like(done)
    scalars = scales(rows)
    block = texts[...].reshape(-1, texts.shape[2])
    other = jnp.concatenate([piece[...] for piece in others], 0).reshape(-1, texts.shape[2])
    size = result.shape[1]
    spans = [slice(index * size, (index + 1) * size) for index in range(result.shape[0])]
    value = coefficients(other, images[...], labels[...], columns[...], scalars)
    stores = []
    for index, span in enumerate(spans):
        total = dot(coef[:, span], block, (0, 0)) + dot(value[:, span], other, (0, 0))
        result[index] = total.astype(result.dtype)
        target = out.at[pl.ds(index * size, size)]
        stores.append(pltpu.make_async_copy(result.at[index], target, out_sems.at[index]))
        stores[-1].start()
    for store in stores:
        store.wait()


def local(images, texts, labels, log_scale, bias, loss_scale):
    far, cores, x, zl = (lax.axis_size(name) for name in ("far", "core", "x", "zl"))
    core = lax.axis_index("core")
    rows = images.shape[0]
    width = texts.shape[1]
    shared = far * x * zl
    frames = rows * shared * cores
    flops = 2 * shared * rows * width

    place = jnp.arange(shared, dtype=jnp.int32)
    first = place // zl % far * (cores * x * zl) + place // (far * zl) * zl + place % zl
    columns = (first + core * x * zl)[:, None]
    columns_other = (first + (1 - core) * x * zl)[:, None]
    half = width // 2
    plane = far * zl

    with jax.named_scope("gather_texts"):
        halves = pl.pallas_call(
            repeat_kernel,
            out_shape=jax.ShapeDtypeStruct((plane, 2, half), texts.dtype),
            in_specs=[VMEM],
            out_specs=VMEM,
            compiler_params=PARAMS,
        )(texts)
        halves = exchange(halves, WIDE)
        blocks = pl.pallas_call(
            spread_kernel,
            out_shape=jax.ShapeDtypeStruct((x, plane, width), texts.dtype),
            in_specs=[VMEM],
            out_specs=VMEM,
            compiler_params=PARAMS,
        )(halves)
        blocks = exchange(blocks, "x")

    with jax.named_scope("swap_images"):
        size = rows // IN_PIECES + TAIL
        *pieces, scale_rows = pl.pallas_call(
            functools.partial(split_kernel, frames=frames),
            out_shape=[pltpu.HBM((size, width), images.dtype)] * IN_PIECES
            + [jax.ShapeDtypeStruct((8, 128), jnp.float32)],
            in_specs=[SMEM] * 3 + [VMEM] * 3,
            out_specs=[HBM] * IN_PIECES + [VMEM],
            scratch_shapes=[
                pltpu.VMEM((IN_PIECES, TAIL, width), images.dtype),
                pltpu.SemaphoreType.DMA((IN_PIECES,)),
                pltpu.SemaphoreType.DMA((IN_PIECES,)),
            ],
            compiler_params=PARAMS,
            cost_estimate=cost(0, 4 * rows * width),
        )(log_scale, bias, loss_scale, *put(pltpu.VMEM, images), labels[None, :], halves)
        others = swap_cores(*pieces)

    with jax.named_scope("coefficients"):
        blocks = hold(blocks)
        coef, part, *copies = pl.pallas_call(
            text_kernel,
            out_shape=(
                jax.ShapeDtypeStruct((shared, rows), jnp.bfloat16),
                jax.ShapeDtypeStruct((shared, width), jnp.bfloat16),
                *[pltpu.HBM((x // TEXT_PIECES, plane, width), blocks.dtype)] * TEXT_PIECES,
            ),
            in_specs=[VMEM] * 4 + [HBM] + [VMEM] * IN_PIECES,
            out_specs=(VMEM, VMEM) + (HBM,) * TEXT_PIECES,
            scratch_shapes=[
                pltpu.VMEM((rows, width), images.dtype),
                pltpu.SemaphoreType.DMA,
                pltpu.SemaphoreType.DMA((TEXT_PIECES,)),
            ],
            compiler_params=PARAMS,
            cost_estimate=cost(4 * flops, 4 * rows * width, 2 * shared * rows),
        )(
            scale_rows,
            columns,
            *put(pltpu.VMEM, blocks),
            labels[None, :],
            *put(pltpu.HBM, images),
            *put(pltpu.VMEM, *others),
        )

    with jax.named_scope("image_grad"):
        copies = swap_cores(*copies)
        image_grad, done = pl.pallas_call(
            image_kernel,
            out_shape=(
                jax.ShapeDtypeStruct((rows, width), jnp.bfloat16),
                jax.ShapeDtypeStruct((8, 128), jnp.float32),
            ),
            in_specs=[VMEM] * (6 + TEXT_PIECES),
            out_specs=(HBM, VMEM),
            scratch_shapes=[
                pltpu.VMEM((OUT_PIECES, rows // OUT_PIECES, width), jnp.bfloat16),
                pltpu.SemaphoreType.DMA((OUT_PIECES,)),
            ],
            compiler_params=PARAMS,
            cost_estimate=cost(0, 0),
        )(scale_rows, columns_other, labels[None, :], coef, blocks, images, *copies)

    with jax.named_scope("text_grad"):
        blocks_grad = exchange(part.reshape(x, plane, width), "x")
        summed = pl.pallas_call(
            gather_kernel,
            out_shape=jax.ShapeDtypeStruct((plane, 2, half), jnp.bfloat16),
            in_specs=[VMEM, VMEM],
            out_specs=VMEM,
            compiler_params=PARAMS,
        )(blocks_grad, done)
        text_grad = pl.pallas_call(
            sum_kernel,
            out_shape=jax.ShapeDtypeStruct((1, width), jnp.bfloat16),
            in_specs=[VMEM],
            out_specs=VMEM,
            compiler_params=PARAMS,
        )(exchange(summed, WIDE))

    return (image_grad, text_grad)


def solution(mesh):
    blk, grp = mesh.devices.shape
    rows = ("far", "core", "x", "zl")
    fine = Mesh(mesh.devices.reshape(blk // 2, 2, 4, grp // 4), rows)
    placed = (P(rows, None), P(rows, None), P(rows), P(), P(), P())
    return jax.shard_map(
        local,
        mesh=fine,
        in_specs=placed,
        out_specs=(P(rows, None), P(rows, None)),
        check_vma=False,
    )
```

time: 84.4 us -> 82.5 us (0.977)
  blocking collectives: 0 us -> 47 us
  starting transfers between devices: 44.3 us -> 18.4 us
  waiting for transfers between devices: 23.3 us -> 3.76 us
  Pallas kernels: 11.9 us -> 9.18 us
    all_to_all x0 -> x2, blocking collectives: none -> 47 us  [exchange(): return lax.all_to_all(array, axes, 0, 0, tiled=True)]
    all_to_all x4 -> x2, starting transfers between devices: 36 us -> 9.72 us  [exchange(): return lax.all_to_all(array, axes, 0, 0, tiled=True)]
    all_to_all x4 -> x2, waiting for transfers between devices: 23.3 us -> 0.59 us  [exchange(): return lax.all_to_all(array, axes, 0, 0, tiled=True)]
    ppermute x4, waiting for transfers between devices: 0.01 us -> 3.17 us  [swap_cores(): return [lax.ppermute(array, 'core', [(0, 1), (1, 0)]) for array in arrays]]
    pallas_call x2 -> x3, Pallas kernels: 4.89 us -> 3.37 us  [the longest x1 2.31 us: local(): pl.pallas_call(image_kernel, out_shape=(jax.ShapeDtypeStruct((rows, width...]
  transfers between devices with their start and end apart: 8 -> 6, of which waited for: 4 -> 3; matrix products, arithmetic and copies ran while one was open for 0% -> 0% of each run, Pallas kernels for 8% -> 4%
where the time goes in v4:
time: 82.5 us; the launch traced here: 81.8 us
  blocking collectives  47 us (57%)
  starting transfers between devices  18.4 us (22%)
  Pallas kernels  9.18 us (11%)
  waiting for transfers between devices  3.76 us (5%)
  between operations  2.74 us (3%)
    all_to_all x2, blocking collectives, exchange(): return lax.all_to_all(array, axes, 0, 0, tiled=True)  47 us
    all_to_all x2, starting transfers between devices, exchange(): return lax.all_to_all(array, axes, 0, 0, tiled=True)  9.72 us
    ppermute x4, starting transfers between devices, swap_cores(): return [lax.ppermute(array, 'core', [(0, 1), (1, 0)]) for array in arrays]  8.64 us
    pallas_call x1, Pallas kernels, local(): pl.pallas_call(text_kernel, out_shape=(jax.ShapeDtypeStruct((shared, rows...  3.74 us
    ppermute x4, waiting for transfers between devices, swap_cores(): return [lax.ppermute(array, 'core', [(0, 1), (1, 0)]) for array in arrays]  3.17 us
    pallas_call x1, Pallas kernels, local(): pl.pallas_call(image_kernel, out_shape=(jax.ShapeDtypeStruct((rows, width...  2.31 us
  transfers between devices with their start and end apart: 6, of which 3 were waited for; matrix products, arithmetic and copies ran while one was open for 0% of the time, Pallas kernels for 4%

profile of v4, /device:TPU:6, one launch (start us, length us, event | category | flops | bytes accessed | tf_op | source)
XLA Modules:
  0.0 81.8 jit_solution(13290626881532081279)
XLA Ops:
  0.6 0.0 copy-start.3
  0.6 0.7 copy-done.3
  1.3 0.1 gather_texts.2
  1.4 0.0 copy-start
  1.4 0.0 copy-start.2
  1.4 29.7 %all_to_all.20.after.halves = bf16[64,2,576]{2,1,0:T(2,128)(2,1)S(1)} all-to-all(bf16[64,2,576]{2,1,0:T(2,128)(2,1)S(1)} %gather_texts.2), channel_id=1, replica_groups=mesh['far'=16,'core'=2,'x'=4,'zl'=4] {'far','zl'}, dimensions={0} | all-to-all | bytes 294912 | tf_op jit(solution)/shard_map/gather_texts/all_to_all | solution.py:29
  31.2 0.9 %gather_texts.3 = bf16[4,64,1152]{2,1,0:T(8,128)(2,1)} custom-call(bf16[64,2,576]{2,1,0:T(2,128)(2,1)S(1)} %all_to_all.20.after.halves), custom_call_target="tpu_custom_call" | custom-call | tf_op jit(solution)/shard_map/gather_texts/pallas_call | solution.py:204
  32.1 4.8 %all-to-all-start.1 = ((bf16[4,64,1152]{2,1,0:T(8,128)(2,1)}), bf16[4,64,1152]{2,1,0:T(8,128)(2,1)S(1)}, u32[]{:S(2)}, u32[]{:S(2)}) async-start(bf16[4,64,1152]{2,1,0:T(8,128)(2,1)} %gather_texts.3), calls=%async_computation.1 | async-start | bytes 1179648 | tf_op jit(solution)/shard_map/gather_texts/all_to_all | solution.py:29
  38.8 0.1 broadcast_add_fusion.columns
  38.9 0.0 copy-done
  38.9 0.0 copy-done.2
  38.9 1.1 %swap_images.1 = (bf16[272,1152]{1,0:T(8,128)(2,1)}, bf16[272,1152]{1,0:T(8,128)(2,1)}, f32[8,128]{1,0:T(8,128)S(1)}) custom-call(f32[1]{0:T(128)S(6)} %copy.11.log_scale, f32[1]{0:T(128)S(6)} %copy.12.bias, f32[1]{0:T(128)S(6)} %copy.13.loss_scale, bf16[512,1152]{1,0:T(8,128)(2,1)S(1)} %copy-done, s32[1,512]{1,0:T(1,128)S(1)} %bitcast.2, ...), custom_call_target="tpu_custom_call" | custom-call | bytes 2359296 | tf_op jit(solution)/shard_map/swap_images/pallas_call | solution.py:215
  40.0 1.9 %collective-permute-start = (bf16[272,1152]{1,0:T(8,128)(2,1)}, bf16[272,1152]{1,0:T(8,128)(2,1)S(1)}, u32[]{:S(2)}, u32[]{:S(2)}) collective-permute-start(bf16[272,1152]{1,0:T(8,128)(2,1)} %get-tuple-element.12), channel_id=1, source_target_pairs={{0,16},{16,0},{1,17},{17,1},{2,18},{18,2},{3,19},{19,3},{4,20},{20... | collective-permute-start | bytes 1880072 | tf_op jit(solution)/shard_map/swap_images/ppermute | solution.py:25
  41.9 2.4 %collective-permute-start.1 = (bf16[272,1152]{1,0:T(8,128)(2,1)}, bf16[272,1152]{1,0:T(8,128)(2,1)S(1)}, u32[]{:S(2)}, u32[]{:S(2)}) collective-permute-start(bf16[272,1152]{1,0:T(8,128)(2,1)} %get-tuple-element.13), channel_id=1, source_target_pairs={{0,16},{16,0},{1,17},{17,1},{2,18},{18,2},{3,19},{19,3},{4,20},{20... | collective-permute-start | bytes 1880072 | tf_op jit(solution)/shard_map/swap_images/ppermute | solution.py:25
  44.3 0.0 all-to-all-done.1.array
  44.3 0.0 collective-permute-done.refs_0_
  44.3 1.8 %collective-permute-done.1.refs_1_ = bf16[272,1152]{1,0:T(8,128)(2,1)S(1)} collective-permute-done((bf16[272,1152]{1,0:T(8,128)(2,1)}, bf16[272,1152]{1,0:T(8,128)(2,1)S(1)}, u32[]{:S(2)}, u32[]{:S(2)}) %collective-permute-start.1) | collective-permute-done | bytes 626720 | tf_op jit(solution)/shard_map/swap_images/ppermute | solution.py:25
  46.2 3.7 %coefficients.3 = (bf16[256,512]{1,0:T(8,128)(2,1)S(1)}, bf16[256,1152]{1,0:T(8,128)(2,1)}, bf16[2,64,1152]{2,1,0:T(8,128)(2,1)}, bf16[2,64,1152]{2,1,0:T(8,128)(2,1)}) custom-call(f32[8,128]{1,0:T(8,128)S(1)} %get-tuple-element.11.rows, s32[256,1]{1,0:T(8,128)S(1)} %broadcast_add_fusion.columns, bf16[4,64,1152]{2,1,0:T(8,128)(2,1)S(1)} %coefficients.2.texts, ...), custom_call_target="tpu_custom_call" | custom-call | flops 1207959552 | bytes 2359296 | tf_op jit(solution)/shard_map/coefficients/pallas_call | solution.py:233
  49.9 0.0 copy-start.1
  49.9 5.0 %all-to-all-start.2 = ((bf16[4,64,1152]{2,1,0:T(8,128)(2,1)}), bf16[4,64,1152]{2,1,0:T(8,128)(2,1)S(1)}, u32[]{:S(2)}, u32[]{:S(2)}) async-start(bf16[4,64,1152]{2,1,0:T(8,128)(2,1)} %bitcast.1), calls=%async_computation.2 | async-start | bytes 1179648 | tf_op jit(solution)/shard_map/text_grad/all_to_all | solution.py:29
  54.9 1.9 %collective-permute-start.2 = (bf16[2,64,1152]{2,1,0:T(8,128)(2,1)}, bf16[2,64,1152]{2,1,0:T(8,128)(2,1)S(1)}, u32[]{:S(2)}, u32[]{:S(2)}) collective-permute-start(bf16[2,64,1152]{2,1,0:T(8,128)(2,1)} %get-tuple-element.15), channel_id=1, source_target_pairs={{0,16},{16,0},{1,17},{17,1},{2,18},{18,2},{3,19},{19,3},{4,20},{20... | collective-permute-start | bytes 884744 | tf_op jit(solution)/shard_map/image_grad/ppermute | solution.py:25
  56.8 2.4 %collective-permute-start.3 = (bf16[2,64,1152]{2,1,0:T(8,128)(2,1)}, bf16[2,64,1152]{2,1,0:T(8,128)(2,1)S(1)}, u32[]{:S(2)}, u32[]{:S(2)}) collective-permute-start(bf16[2,64,1152]{2,1,0:T(8,128)(2,1)} %get-tuple-element.16), channel_id=1, source_target_pairs={{0,16},{16,0},{1,17},{17,1},{2,18},{18,2},{3,19},{19,3},{4,20},{20... | collective-permute-start | bytes 884744 | tf_op jit(solution)/shard_map/image_grad/ppermute | solution.py:25
  59.2 0.1 broadcast_add_fusion.1.columns
  59.3 0.0 collective-permute-done.2.refs_0_
  59.3 1.3 %collective-permute-done.3.refs_1_ = bf16[2,64,1152]{2,1,0:T(8,128)(2,1)S(1)} collective-permute-done((bf16[2,64,1152]{2,1,0:T(8,128)(2,1)}, bf16[2,64,1152]{2,1,0:T(8,128)(2,1)S(1)}, u32[]{:S(2)}, u32[]{:S(2)}) %collective-permute-start.3) | collective-permute-done | bytes 294944 | tf_op jit(solution)/shard_map/image_grad/ppermute | solution.py:25
  60.6 0.0 copy-done.1
  60.6 2.3 %image_grad.1 = (bf16[512,1152]{1,0:T(8,128)(2,1)}, f32[8,128]{1,0:T(8,128)S(1)}) custom-call(f32[8,128]{1,0:T(8,128)S(1)} %get-tuple-element.11.rows, s32[256,1]{1,0:T(8,128)S(1)} %broadcast_add_fusion.1.columns, s32[1,512]{1,0:T(1,128)S(1)} %bitcast.4, bf16[256,512]{1,0:T(8,128)(2,1)S(1)} %get-tuple-element.14.coef, ...), custom_call_target="tpu_custom_call" | custom-call | tf_op jit(solution)/shard_map/image_grad/pallas_call | solution.py:260
  62.9 0.6 all-to-all-done.2.blocks
  63.5 0.2 text_grad.2
  63.7 17.3 %all_to_all.21.parts = bf16[64,2,576]{2,1,0:T(2,128)(2,1)S(1)} all-to-all(bf16[64,2,576]{2,1,0:T(2,128)(2,1)S(1)} %text_grad.2), channel_id=1, replica_groups=mesh['far'=16,'core'=2,'x'=4,'zl'=4] {'far','zl'}, dimensions={0} | all-to-all | bytes 294912 | tf_op jit(solution)/shard_map/text_grad/all_to_all | solution.py:29
  81.0 0.8 %text_grad.3 = bf16[1,1152]{1,0:T(2,128)(2,1)} custom-call(bf16[64,2,576]{2,1,0:T(2,128)(2,1)S(1)} %all_to_all.21.parts), custom_call_target="tpu_custom_call" | custom-call | tf_op jit(solution)/shard_map/text_grad/pallas_call | solution.py:285
  (1 shorter events, 0.0 us)
Async XLA Ops:
  0.6 0.7 copy-start.3
  1.4 37.5 %copy-start = (bf16[512,1152]{1,0:T(8,128)(2,1)S(1)}, bf16[512,1152]{1,0:T(8,128)(2,1)}, u32[]{:S(2)}) copy-start(bf16[512,1152]{1,0:T(8,128)(2,1)} %images.3) | copy-start | bytes 3538948
  1.4 37.5 %copy-start.2 = (s32[512]{0:T(512)S(1)}, s32[512]{0:T(512)}, u32[]{:S(2)}) copy-start(s32[512]{0:T(512)} %param.8) | copy-start | bytes 6148
  32.1 12.2 %all-to-all-start.1 = ((bf16[4,64,1152]{2,1,0:T(8,128)(2,1)}), bf16[4,64,1152]{2,1,0:T(8,128)(2,1)S(1)}, u32[]{:S(2)}, u32[]{:S(2)}) async-start(bf16[4,64,1152]{2,1,0:T(8,128)(2,1)} %gather_texts.3), calls=%async_computation.1 | async-start | bytes 1179648 | tf_op jit(solution)/shard_map/gather_texts/all_to_all | solution.py:29
  40.0 4.4 %collective-permute-start = (bf16[272,1152]{1,0:T(8,128)(2,1)}, bf16[272,1152]{1,0:T(8,128)(2,1)S(1)}, u32[]{:S(2)}, u32[]{:S(2)}) collective-permute-start(bf16[272,1152]{1,0:T(8,128)(2,1)} %get-tuple-element.12), channel_id=1, source_target_pairs={{0,16},{16,0},{1,17},{17,1},{2,18},{18,2},{3,19},{19,3},{4,20},{20... | collective-permute-start | bytes 1880072 | tf_op jit(solution)/shard_map/swap_images/ppermute | solution.py:25
  41.9 4.3 %collective-permute-start.1 = (bf16[272,1152]{1,0:T(8,128)(2,1)}, bf16[272,1152]{1,0:T(8,128)(2,1)S(1)}, u32[]{:S(2)}, u32[]{:S(2)}) collective-permute-start(bf16[272,1152]{1,0:T(8,128)(2,1)} %get-tuple-element.13), channel_id=1, source_target_pairs={{0,16},{16,0},{1,17},{17,1},{2,18},{18,2},{3,19},{19,3},{4,20},{20... | collective-permute-start | bytes 1880072 | tf_op jit(solution)/shard_map/swap_images/ppermute | solution.py:25
  49.9 10.7 %copy-start.1 = (bf16[512,1152]{1,0:T(8,128)(2,1)S(1)}, bf16[512,1152]{1,0:T(8,128)(2,1)}, u32[]{:S(2)}) copy-start(bf16[512,1152]{1,0:T(8,128)(2,1)} %images.3) | copy-start | bytes 3538948
  49.9 13.6 %all-to-all-start.2 = ((bf16[4,64,1152]{2,1,0:T(8,128)(2,1)}), bf16[4,64,1152]{2,1,0:T(8,128)(2,1)S(1)}, u32[]{:S(2)}, u32[]{:S(2)}) async-start(bf16[4,64,1152]{2,1,0:T(8,128)(2,1)} %bitcast.1), calls=%async_computation.2 | async-start | bytes 1179648 | tf_op jit(solution)/shard_map/text_grad/all_to_all | solution.py:29
  54.9 4.4 %collective-permute-start.2 = (bf16[2,64,1152]{2,1,0:T(8,128)(2,1)}, bf16[2,64,1152]{2,1,0:T(8,128)(2,1)S(1)}, u32[]{:S(2)}, u32[]{:S(2)}) collective-permute-start(bf16[2,64,1152]{2,1,0:T(8,128)(2,1)} %get-tuple-element.15), channel_id=1, source_target_pairs={{0,16},{16,0},{1,17},{17,1},{2,18},{18,2},{3,19},{19,3},{4,20},{20... | collective-permute-start | bytes 884744 | tf_op jit(solution)/shard_map/image_grad/ppermute | solution.py:25
  56.8 3.8 %collective-permute-start.3 = (bf16[2,64,1152]{2,1,0:T(8,128)(2,1)}, bf16[2,64,1152]{2,1,0:T(8,128)(2,1)S(1)}, u32[]{:S(2)}, u32[]{:S(2)}) collective-permute-start(bf16[2,64,1152]{2,1,0:T(8,128)(2,1)} %get-tuple-element.16), channel_id=1, source_target_pairs={{0,16},{16,0},{1,17},{17,1},{2,18},{18,2},{3,19},{19,3},{4,20},{20... | collective-permute-start | bytes 884744 | tf_op jit(solution)/shard_map/image_grad/ppermute | solution.py:25

commit v5 on v4

--- a/solution.py
+++ b/solution.py
@@ -73,22 +73,6 @@
     out[:, width:] = total[1:2].astype(out.dtype)
 
 
-def hold_kernel(array, out):
-    del array, out
-
-
-def hold(array):
-    return pl.pallas_call(
-        hold_kernel,
-        out_shape=jax.ShapeDtypeStruct(array.shape, array.dtype),
-        in_specs=[ANY],
-        out_specs=ANY,
-        input_output_aliases={0: 0},
-        compiler_params=PARAMS,
-        cost_estimate=cost(HOLD, 0),
-    )(array)
-
-
 def split_kernel(log_scale, bias, loss_scale, whole, labels, after, *refs, frames):
     del after
     *pieces, rows, tails, sems, tail_sems = refs
@@ -128,16 +112,21 @@
     return rows[0:1, 0:1], rows[1:2, 0:1], rows[2:3, 0:1]
 
 
-def text_kernel(rows, columns, texts, labels, images, *refs):
-    others, (coef, part, *copies, held, load_sem, sems) = refs[:IN_PIECES], refs[IN_PIECES:]
-    load = pltpu.make_async_copy(images, held, load_sem)
-    load.start()
+def own_kernel(rows, columns, texts, labels, images, coef, *refs):
+    *copies, sems = refs
     stores = []
     for index, copy in enumerate(copies):
         source = texts.at[pl.ds(index * copy.shape[0], copy.shape[0])]
         stores.append(pltpu.make_async_copy(source, copy, sems.at[index]))
         stores[-1].start()
-    scalars = scales(rows)
+    block = texts[...].reshape(-1, texts.shape[2])
+    coef[...] = coefficients(block, images[...], labels[...], columns[...], scales(rows))
+    for store in stores:
+        store.wait()
+
+
+def text_kernel(rows, columns, texts, coef, images, *refs):
+    *others, part = refs
     block = texts[...].reshape(part.shape)
     terms = []
     for piece in others:
@@ -145,15 +134,10 @@
         frames = piece[:size, :]
         tail = piece[size:, :size].astype(jnp.float32)
         paired = (tail[0:1] * 32 + tail[1:2]).astype(jnp.int32)
-        terms.append((coefficients(block, frames, paired, columns[...], scalars), frames))
-    load.wait()
-    value = coefficients(block, held[...], labels[...], columns[...], scalars)
-    coef[...] = value
-    terms.append((value, held[...]))
+        terms.append((coefficients(block, frames, paired, columns[...], scales(rows)), frames))
+    terms.append((coef[...], images[...]))
     total = sum(dot(value, frames, (1, 0)) for value, frames in terms)
     part[...] = total.astype(part.dtype)
-    for store in stores:
-        store.wait()
 
 
 def image_kernel(rows, columns, labels, coef, texts, images, *refs):
@@ -229,30 +213,29 @@
         others = swap_cores(*pieces)
 
     with jax.named_scope("coefficients"):
-        blocks = hold(blocks)
-        coef, part, *copies = pl.pallas_call(
-            text_kernel,
+        coef, *copies = pl.pallas_call(
+            own_kernel,
             out_shape=(
                 jax.ShapeDtypeStruct((shared, rows), jnp.bfloat16),
-                jax.ShapeDtypeStruct((shared, width), jnp.bfloat16),
                 *[pltpu.HBM((x // TEXT_PIECES, plane, width), blocks.dtype)] * TEXT_PIECES,
             ),
-            in_specs=[VMEM] * 4 + [HBM] + [VMEM] * IN_PIECES,
-            out_specs=(VMEM, VMEM) + (HBM,) * TEXT_PIECES,
-            scratch_shapes=[
-                pltpu.VMEM((rows, width), images.dtype),
-                pltpu.SemaphoreType.DMA,
-                pltpu.SemaphoreType.DMA((TEXT_PIECES,)),
-            ],
-            compiler_params=PARAMS,
-            cost_estimate=cost(4 * flops, 4 * rows * width, 2 * shared * rows),
+            in_specs=[VMEM] * 5,
+            out_specs=(VMEM,) + (HBM,) * TEXT_PIECES,
+            scratch_shapes=[pltpu.SemaphoreType.DMA((TEXT_PIECES,))],
+            compiler_params=PARAMS,
+            cost_estimate=cost(HOLD, 4 * rows * width, shared * rows),
+        )(scale_rows, columns, *put(pltpu.VMEM, blocks), labels[None, :], *put(pltpu.VMEM, images))
+        part = pl.pallas_call(
+            text_kernel,
+            out_shape=jax.ShapeDtypeStruct((shared, width), jnp.bfloat16),
+            in_specs=[VMEM] * (5 + IN_PIECES),
+            out_specs=VMEM,
+            compiler_params=PARAMS,
+            cost_estimate=cost(3 * flops, 4 * rows * width, shared * rows),
         )(
             scale_rows,
             columns,
-            *put(pltpu.VMEM, blocks),
-            labels[None, :],
-            *put(pltpu.HBM, images),
-            *put(pltpu.VMEM, *others),
+            *put(pltpu.VMEM, blocks, coef, images, *others),
         )
 
     with jax.named_scope("image_grad"):

time: 82.5 us -> 82.2 us (level)
  waiting for transfers between devices: 3.76 us -> 2.85 us
    ppermute x4, waiting for transfers between devices: 3.17 us -> 2.04 us  [swap_cores(): return [lax.ppermute(array, 'core', [(0, 1), (1, 0)]) for array in arrays]]
  transfers between devices with their start and end apart: 6 -> 6, of which waited for: 3 -> 3; matrix products, arithmetic and copies ran while one was open for 0% -> 0% of each run, Pallas kernels for 4% -> 5%
where the time goes in v5:
time: 82.2 us; the launch traced here: 81.3 us
  blocking collectives  46.8 us (57%)
  starting transfers between devices  18.4 us (22%)
  Pallas kernels  9.76 us (12%)
  waiting for transfers between devices  2.85 us (3%)
  between operations  2.73 us (3%)
    all_to_all x2, blocking collectives, exchange(): return lax.all_to_all(array, axes, 0, 0, tiled=True)  46.8 us
    all_to_all x2, starting transfers between devices, exchange(): return lax.all_to_all(array, axes, 0, 0, tiled=True)  9.71 us
    ppermute x4, starting transfers between devices, swap_cores(): return [lax.ppermute(array, 'core', [(0, 1), (1, 0)]) for array in arrays]  8.64 us
    pallas_call x1, Pallas kernels, local(): pl.pallas_call(text_kernel, out_shape=jax.ShapeDtypeStruct((shared, width...  3.27 us
    pallas_call x1, Pallas kernels, local(): pl.pallas_call(image_kernel, out_shape=(jax.ShapeDtypeStruct((rows, width...  2.3 us
    ppermute x4, waiting for transfers between devices, swap_cores(): return [lax.ppermute(array, 'core', [(0, 1), (1, 0)]) for array in arrays]  2.04 us
  transfers between devices with their start and end apart: 6, of which 3 were waited for; matrix products, arithmetic and copies ran while one was open for 0% of the time, Pallas kernels for 5%

profile of v5, /device:TPU:6, one launch (start us, length us, event | category | flops | bytes accessed | tf_op | source)
XLA Modules:
  0.0 81.3 jit_solution(17155780901578240210)
XLA Ops:
  0.6 0.0 copy-start.2
  0.6 0.7 copy-done.2
  1.3 0.1 gather_texts.2
  1.4 0.0 copy-start
  1.4 0.0 copy-start.1
  1.4 29.7 %all_to_all.20.after.halves = bf16[64,2,576]{2,1,0:T(2,128)(2,1)S(1)} all-to-all(bf16[64,2,576]{2,1,0:T(2,128)(2,1)S(1)} %gather_texts.2), channel_id=1, replica_groups=mesh['far'=16,'core'=2,'x'=4,'zl'=4] {'far','zl'}, dimensions={0} | all-to-all | bytes 294912 | tf_op jit(solution)/shard_map/gather_texts/all_to_all | solution.py:29
  31.2 0.9 %gather_texts.3 = bf16[4,64,1152]{2,1,0:T(8,128)(2,1)} custom-call(bf16[64,2,576]{2,1,0:T(2,128)(2,1)S(1)} %all_to_all.20.after.halves), custom_call_target="tpu_custom_call" | custom-call | tf_op jit(solution)/shard_map/gather_texts/pallas_call | solution.py:188
  32.1 4.8 %all-to-all-start.1 = ((bf16[4,64,1152]{2,1,0:T(8,128)(2,1)}), bf16[4,64,1152]{2,1,0:T(8,128)(2,1)S(1)}, u32[]{:S(2)}, u32[]{:S(2)}) async-start(bf16[4,64,1152]{2,1,0:T(8,128)(2,1)} %gather_texts.3), calls=%async_computation.1 | async-start | bytes 1179648 | tf_op jit(solution)/shard_map/gather_texts/all_to_all | solution.py:29
  38.8 0.1 broadcast_add_fusion.columns
  38.9 0.0 copy-done
  38.9 0.0 copy-done.1
  38.9 1.1 %swap_images.1 = (bf16[272,1152]{1,0:T(8,128)(2,1)}, bf16[272,1152]{1,0:T(8,128)(2,1)}, f32[8,128]{1,0:T(8,128)S(1)}) custom-call(f32[1]{0:T(128)S(6)} %copy.8.log_scale, f32[1]{0:T(128)S(6)} %copy.9.bias, f32[1]{0:T(128)S(6)} %copy.10.loss_scale, bf16[512,1152]{1,0:T(8,128)(2,1)S(1)} %copy-done, s32[1,512]{1,0:T(1,128)S(1)} %bitcast.2, ...), custom_call_target="tpu_custom_call" | custom-call | bytes 2359296 | tf_op jit(solution)/shard_map/swap_images/pallas_call | solution.py:199
  40.0 1.9 %collective-permute-start.2 = (bf16[272,1152]{1,0:T(8,128)(2,1)}, bf16[272,1152]{1,0:T(8,128)(2,1)S(1)}, u32[]{:S(2)}, u32[]{:S(2)}) collective-permute-start(bf16[272,1152]{1,0:T(8,128)(2,1)} %get-tuple-element.15), channel_id=1, source_target_pairs={{0,16},{16,0},{1,17},{17,1},{2,18},{18,2},{3,19},{19,3},{4,20},{20... | collective-permute-start | bytes 1880072 | tf_op jit(solution)/shard_map/swap_images/ppermute | solution.py:25
  41.9 2.4 %collective-permute-start.3 = (bf16[272,1152]{1,0:T(8,128)(2,1)}, bf16[272,1152]{1,0:T(8,128)(2,1)}, u32[]{:S(2)}, u32[]{:S(2)}) collective-permute-start(bf16[272,1152]{1,0:T(8,128)(2,1)} %get-tuple-element.16), channel_id=1, source_target_pairs={{0,16},{16,0},{1,17},{17,1},{2,18},{18,2},{3,19},{19,3},{4,20},{20... | collective-permute-start | bytes 1880072 | tf_op jit(solution)/shard_map/swap_images/ppermute | solution.py:25
  44.3 0.0 all-to-all-done.1.texts
  44.3 1.1 %coefficients.2 = (bf16[256,512]{1,0:T(8,128)(2,1)S(1)}, bf16[2,64,1152]{2,1,0:T(8,128)(2,1)}, bf16[2,64,1152]{2,1,0:T(8,128)(2,1)}) custom-call(f32[8,128]{1,0:T(8,128)S(1)} %get-tuple-element.10.rows, s32[256,1]{1,0:T(8,128)S(1)} %broadcast_add_fusion.columns, bf16[4,64,1152]{2,1,0:T(8,128)(2,1)S(1)} %all-to-all-done.1.texts, s32[1,512]{1,0:T(1,128)S(1)} %bitcast.3, ...), custom_call_target="tpu_custom_call" | custom-call | flops 17179869184 | bytes 2359296 | tf_op jit(solution)/shard_map/coefficients/pallas_call | solution.py:216
  45.4 0.0 collective-permute-done.2.refs_0_
  45.4 0.9 %collective-permute-done.3.refs_1_ = bf16[272,1152]{1,0:T(8,128)(2,1)} collective-permute-done((bf16[272,1152]{1,0:T(8,128)(2,1)}, bf16[272,1152]{1,0:T(8,128)(2,1)}, u32[]{:S(2)}, u32[]{:S(2)}) %collective-permute-start.3) | collective-permute-done | bytes 626720 | tf_op jit(solution)/shard_map/swap_images/ppermute | solution.py:25
  46.3 3.3 %coefficients.3 = bf16[256,1152]{1,0:T(8,128)(2,1)} custom-call(f32[8,128]{1,0:T(8,128)S(1)} %get-tuple-element.10.rows, s32[256,1]{1,0:T(8,128)S(1)} %broadcast_add_fusion.columns, bf16[4,64,1152]{2,1,0:T(8,128)(2,1)S(1)} %all-to-all-done.1.texts, bf16[256,512]{1,0:T(8,128)(2,1)S(1)} %get-tuple-element.11.coef, bf16[512,1152]{1,0:T(8,128)(2,1)S(1)} %copy-done, ...), custom_call_target="tpu_custom_call" | custom-call | flops 905969664 | bytes 2359296 | tf_op jit(solution)/shard_map/coefficients/pallas_call | solution.py:228
  49.6 0.0 copy-start.3
  49.6 4.9 %all-to-all-start.2 = ((bf16[4,64,1152]{2,1,0:T(8,128)(2,1)}), bf16[4,64,1152]{2,1,0:T(8,128)(2,1)S(1)}, u32[]{:S(2)}, u32[]{:S(2)}) async-start(bf16[4,64,1152]{2,1,0:T(8,128)(2,1)} %bitcast.1), calls=%async_computation.2 | async-start | bytes 1179648 | tf_op jit(solution)/shard_map/text_grad/all_to_all | solution.py:29
  54.5 1.9 %collective-permute-start = (bf16[2,64,1152]{2,1,0:T(8,128)(2,1)}, bf16[2,64,1152]{2,1,0:T(8,128)(2,1)S(1)}, u32[]{:S(2)}, u32[]{:S(2)}) collective-permute-start(bf16[2,64,1152]{2,1,0:T(8,128)(2,1)} %get-tuple-element.12), channel_id=1, source_target_pairs={{0,16},{16,0},{1,17},{17,1},{2,18},{18,2},{3,19},{19,3},{4,20},{20... | collective-permute-start | bytes 884744 | tf_op jit(solution)/shard_map/image_grad/ppermute | solution.py:25
  56.5 0.0 copy-done.3
  56.5 2.4 %collective-permute-start.1 = (bf16[2,64,1152]{2,1,0:T(8,128)(2,1)S(1)}, bf16[2,64,1152]{2,1,0:T(8,128)(2,1)S(1)}, u32[]{:S(2)}, u32[]{:S(2)}) collective-permute-start(bf16[2,64,1152]{2,1,0:T(8,128)(2,1)S(1)} %copy-done.3), channel_id=1, source_target_pairs={{0,16},{16,0},{1,17},{17,1},{2,18},{18,2},{3,19},{19,3},{4,20},{20... | collective-permute-start | bytes 884744 | tf_op jit(solution)/shard_map/image_grad/ppermute | solution.py:25
  58.9 0.1 broadcast_add_fusion.1.columns
  58.9 0.0 collective-permute-done.refs_0_
  59.0 1.1 %collective-permute-done.1.refs_1_ = bf16[2,64,1152]{2,1,0:T(8,128)(2,1)S(1)} collective-permute-done((bf16[2,64,1152]{2,1,0:T(8,128)(2,1)S(1)}, bf16[2,64,1152]{2,1,0:T(8,128)(2,1)S(1)}, u32[]{:S(2)}, u32[]{:S(2)}) %collective-permute-start.1) | collective-permute-done | bytes 294944 | tf_op jit(solution)/shard_map/image_grad/ppermute | solution.py:25
  60.1 2.3 %image_grad.1 = (bf16[512,1152]{1,0:T(8,128)(2,1)}, f32[8,128]{1,0:T(8,128)S(1)}) custom-call(f32[8,128]{1,0:T(8,128)S(1)} %get-tuple-element.10.rows, s32[256,1]{1,0:T(8,128)S(1)} %broadcast_add_fusion.1.columns, s32[1,512]{1,0:T(1,128)S(1)} %bitcast.4, bf16[256,512]{1,0:T(8,128)(2,1)S(1)} %get-tuple-element.11.coef, ...), custom_call_target="tpu_custom_call" | custom-call | tf_op jit(solution)/shard_map/image_grad/pallas_call | solution.py:243
  62.4 0.8 all-to-all-done.2.blocks
  63.2 0.2 text_grad.2
  63.4 17.1 %all_to_all.21.parts = bf16[64,2,576]{2,1,0:T(2,128)(2,1)S(1)} all-to-all(bf16[64,2,576]{2,1,0:T(2,128)(2,1)S(1)} %text_grad.2), channel_id=1, replica_groups=mesh['far'=16,'core'=2,'x'=4,'zl'=4] {'far','zl'}, dimensions={0} | all-to-all | bytes 294912 | tf_op jit(solution)/shard_map/text_grad/all_to_all | solution.py:29
  80.4 0.8 %text_grad.3 = bf16[1,1152]{1,0:T(2,128)(2,1)} custom-call(bf16[64,2,576]{2,1,0:T(2,128)(2,1)S(1)} %all_to_all.21.parts), custom_call_target="tpu_custom_call" | custom-call | tf_op jit(solution)/shard_map/text_grad/pallas_call | solution.py:268
Async XLA Ops:
  0.6 0.7 copy-start.2
  1.4 37.5 %copy-start = (bf16[512,1152]{1,0:T(8,128)(2,1)S(1)}, bf16[512,1152]{1,0:T(8,128)(2,1)}, u32[]{:S(2)}) copy-start(bf16[512,1152]{1,0:T(8,128)(2,1)} %images.5) | copy-start | bytes 3538948
  1.4 37.5 %copy-start.1 = (s32[512]{0:T(512)S(1)}, s32[512]{0:T(512)}, u32[]{:S(2)}) copy-start(s32[512]{0:T(512)} %param.8) | copy-start | bytes 6148
  32.1 12.2 %all-to-all-start.1 = ((bf16[4,64,1152]{2,1,0:T(8,128)(2,1)}), bf16[4,64,1152]{2,1,0:T(8,128)(2,1)S(1)}, u32[]{:S(2)}, u32[]{:S(2)}) async-start(bf16[4,64,1152]{2,1,0:T(8,128)(2,1)} %gather_texts.3), calls=%async_computation.1 | async-start | bytes 1179648 | tf_op jit(solution)/shard_map/gather_texts/all_to_all | solution.py:29
  40.0 5.4 %collective-permute-start.2 = (bf16[272,1152]{1,0:T(8,128)(2,1)}, bf16[272,1152]{1,0:T(8,128)(2,1)S(1)}, u32[]{:S(2)}, u32[]{:S(2)}) collective-permute-start(bf16[272,1152]{1,0:T(8,128)(2,1)} %get-tuple-element.15), channel_id=1, source_target_pairs={{0,16},{16,0},{1,17},{17,1},{2,18},{18,2},{3,19},{19,3},{4,20},{20... | collective-permute-start | bytes 1880072 | tf_op jit(solution)/shard_map/swap_images/ppermute | solution.py:25
  41.9 4.4 %collective-permute-start.3 = (bf16[272,1152]{1,0:T(8,128)(2,1)}, bf16[272,1152]{1,0:T(8,128)(2,1)}, u32[]{:S(2)}, u32[]{:S(2)}) collective-permute-start(bf16[272,1152]{1,0:T(8,128)(2,1)} %get-tuple-element.16), channel_id=1, source_target_pairs={{0,16},{16,0},{1,17},{17,1},{2,18},{18,2},{3,19},{19,3},{4,20},{20... | collective-permute-start | bytes 1880072 | tf_op jit(solution)/shard_map/swap_images/ppermute | solution.py:25
  49.6 6.9 %copy-start.3 = (bf16[2,64,1152]{2,1,0:T(8,128)(2,1)S(1)}, bf16[2,64,1152]{2,1,0:T(8,128)(2,1)}, u32[]{:S(2)}) copy-start(bf16[2,64,1152]{2,1,0:T(8,128)(2,1)} %get-tuple-element.13) | copy-start | bytes 884740
  49.6 13.6 %all-to-all-start.2 = ((bf16[4,64,1152]{2,1,0:T(8,128)(2,1)}), bf16[4,64,1152]{2,1,0:T(8,128)(2,1)S(1)}, u32[]{:S(2)}, u32[]{:S(2)}) async-start(bf16[4,64,1152]{2,1,0:T(8,128)(2,1)} %bitcast.1), calls=%async_computation.2 | async-start | bytes 1179648 | tf_op jit(solution)/shard_map/text_grad/all_to_all | solution.py:29
  54.5 4.4 %collective-permute-start = (bf16[2,64,1152]{2,1,0:T(8,128)(2,1)}, bf16[2,64,1152]{2,1,0:T(8,128)(2,1)S(1)}, u32[]{:S(2)}, u32[]{:S(2)}) collective-permute-start(bf16[2,64,1152]{2,1,0:T(8,128)(2,1)} %get-tuple-element.12), channel_id=1, source_target_pairs={{0,16},{16,0},{1,17},{17,1},{2,18},{18,2},{3,19},{19,3},{4,20},{20... | collective-permute-start | bytes 884744 | tf_op jit(solution)/shard_map/image_grad/ppermute | solution.py:25
  56.5 3.6 %collective-permute-start.1 = (bf16[2,64,1152]{2,1,0:T(8,128)(2,1)S(1)}, bf16[2,64,1152]{2,1,0:T(8,128)(2,1)S(1)}, u32[]{:S(2)}, u32[]{:S(2)}) collective-permute-start(bf16[2,64,1152]{2,1,0:T(8,128)(2,1)S(1)} %copy-done.3), channel_id=1, source_target_pairs={{0,16},{16,0},{1,17},{17,1},{2,18},{18,2},{3,19},{19,3},{4,20},{20... | collective-permute-start | bytes 884744 | tf_op jit(solution)/shard_map/image_grad/ppermute | solution.py:25

commit v6 on v5

--- a/solution.py
+++ b/solution.py
@@ -73,9 +73,9 @@
     out[:, width:] = total[1:2].astype(out.dtype)
 
 
-def split_kernel(log_scale, bias, loss_scale, whole, labels, after, *refs, frames):
+def split_kernel(whole, labels, after, *refs):
     del after
-    *pieces, rows, tails, sems, tail_sems = refs
+    *pieces, tails, sems, tail_sems = refs
     size = pieces[0].shape[0] - TAIL
     stores = []
     for index, piece in enumerate(pieces):
@@ -92,10 +92,6 @@
         target = piece.at[pl.ds(size, TAIL)]
         stores.append(pltpu.make_async_copy(tails.at[index], target, tail_sems.at[index]))
         stores[-1].start()
-    factor = jnp.exp(jnp.full((1, rows.shape[1]), log_scale[0]))
-    rows[0:1, :] = factor
-    rows[1:2, :] = jnp.full(factor.shape, bias[0])
-    rows[2:3, :] = factor * loss_scale[0] / frames
     for store in stores:
         store.wait()
 
@@ -112,13 +108,19 @@
     return rows[0:1, 0:1], rows[1:2, 0:1], rows[2:3, 0:1]
 
 
-def own_kernel(rows, columns, texts, labels, images, coef, *refs):
+def own_kernel(
+    log_scale, bias, loss_scale, columns, texts, labels, images, coef, rows, *refs, frames
+):
     *copies, sems = refs
     stores = []
     for index, copy in enumerate(copies):
         source = texts.at[pl.ds(index * copy.shape[0], copy.shape[0])]
         stores.append(pltpu.make_async_copy(source, copy, sems.at[index]))
         stores[-1].start()
+    factor = jnp.exp(jnp.full((1, rows.shape[1]), log_scale[0]))
+    rows[0:1, :] = factor
+    rows[1:2, :] = jnp.full(factor.shape, bias[0])
+    rows[2:3, :] = factor * loss_scale[0] / frames
     block = texts[...].reshape(-1, texts.shape[2])
     coef[...] = coefficients(block, images[...], labels[...], columns[...], scales(rows))
     for store in stores:
@@ -196,12 +198,11 @@
 
     with jax.named_scope("swap_images"):
         size = rows // IN_PIECES + TAIL
-        *pieces, scale_rows = pl.pallas_call(
-            functools.partial(split_kernel, frames=frames),
-            out_shape=[pltpu.HBM((size, width), images.dtype)] * IN_PIECES
-            + [jax.ShapeDtypeStruct((8, 128), jnp.float32)],
-            in_specs=[SMEM] * 3 + [VMEM] * 3,
-            out_specs=[HBM] * IN_PIECES + [VMEM],
+        pieces = pl.pallas_call(
+            split_kernel,
+            out_shape=[pltpu.HBM((size, width), images.dtype)] * IN_PIECES,
+            in_specs=[VMEM] * 3,
+            out_specs=[HBM] * IN_PIECES,
             scratch_shapes=[
                 pltpu.VMEM((IN_PIECES, TAIL, width), images.dtype),
                 pltpu.SemaphoreType.DMA((IN_PIECES,)),
@@ -209,22 +210,31 @@
             ],
             compiler_params=PARAMS,
             cost_estimate=cost(0, 4 * rows * width),
-        )(log_scale, bias, loss_scale, *put(pltpu.VMEM, images), labels[None, :], halves)
+        )(*put(pltpu.VMEM, images), labels[None, :], halves)
         others = swap_cores(*pieces)
 
     with jax.named_scope("coefficients"):
-        coef, *copies = pl.pallas_call(
-            own_kernel,
+        coef, scale_rows, *copies = pl.pallas_call(
+            functools.partial(own_kernel, frames=frames),
             out_shape=(
                 jax.ShapeDtypeStruct((shared, rows), jnp.bfloat16),
+                jax.ShapeDtypeStruct((8, 128), jnp.float32),
                 *[pltpu.HBM((x // TEXT_PIECES, plane, width), blocks.dtype)] * TEXT_PIECES,
             ),
-            in_specs=[VMEM] * 5,
-            out_specs=(VMEM,) + (HBM,) * TEXT_PIECES,
+            in_specs=[SMEM] * 3 + [VMEM] * 4,
+            out_specs=(VMEM, VMEM) + (HBM,) * TEXT_PIECES,
             scratch_shapes=[pltpu.SemaphoreType.DMA((TEXT_PIECES,))],
             compiler_params=PARAMS,
             cost_estimate=cost(HOLD, 4 * rows * width, shared * rows),
-        )(scale_rows, columns, *put(pltpu.VMEM, blocks), labels[None, :], *put(pltpu.VMEM, images))
+        )(
+            log_scale,
+            bias,
+            loss_scale,
+            columns,
+            *put(pltpu.VMEM, blocks),
+            labels[None, :],
+            *put(pltpu.VMEM, images),
+        )
         part = pl.pallas_call(
             text_kernel,
             out_shape=jax.ShapeDtypeStruct((shared, width), jnp.bfloat16),

time: 82.2 us -> 82.2 us (level)
  no operation moved by 1% of the time
where the time goes in v6:
time: 82.2 us; the launch traced here: 81.3 us
  blocking collectives  46.8 us (57%)
  starting transfers between devices  18.4 us (22%)
  Pallas kernels  9.76 us (12%)
  waiting for transfers between devices  2.84 us (3%)
  between operations  2.73 us (3%)
    all_to_all x2, blocking collectives, exchange(): return lax.all_to_all(array, axes, 0, 0, tiled=True)  46.8 us
    all_to_all x2, starting transfers between devices, exchange(): return lax.all_to_all(array, axes, 0, 0, tiled=True)  9.71 us
    ppermute x4, starting transfers between devices, swap_cores(): return [lax.ppermute(array, 'core', [(0, 1), (1, 0)]) for array in arrays]  8.64 us
    pallas_call x1, Pallas kernels, local(): pl.pallas_call(text_kernel, out_shape=jax.ShapeDtypeStruct((shared, width...  3.27 us
    pallas_call x1, Pallas kernels, local(): pl.pallas_call(image_kernel, out_shape=(jax.ShapeDtypeStruct((rows, width...  2.3 us
    ppermute x4, waiting for transfers between devices, swap_cores(): return [lax.ppermute(array, 'core', [(0, 1), (1, 0)]) for array in arrays]  2.04 us
  transfers between devices with their start and end apart: 6, of which 3 were waited for; matrix products, arithmetic and copies ran while one was open for 0% of the time, Pallas kernels for 5%

profile of v6, /device:TPU:6, one launch (start us, length us, event | category | flops | bytes accessed | tf_op | source)
XLA Modules:
  0.0 81.3 jit_solution(188152720496418598)
XLA Ops:
  0.6 0.0 copy-start.2
  0.6 0.7 copy-done.2
  1.3 0.1 gather_texts.2
  1.4 0.0 copy-start
  1.4 0.0 copy-start.1
  1.4 29.7 %all_to_all.20.halves.after = bf16[64,2,576]{2,1,0:T(2,128)(2,1)S(1)} all-to-all(bf16[64,2,576]{2,1,0:T(2,128)(2,1)S(1)} %gather_texts.2), channel_id=1, replica_groups=mesh['far'=16,'core'=2,'x'=4,'zl'=4] {'far','zl'}, dimensions={0} | all-to-all | bytes 294912 | tf_op jit(solution)/shard_map/gather_texts/all_to_all | solution.py:29
  31.2 0.9 %gather_texts.3 = bf16[4,64,1152]{2,1,0:T(8,128)(2,1)} custom-call(bf16[64,2,576]{2,1,0:T(2,128)(2,1)S(1)} %all_to_all.20.halves.after), custom_call_target="tpu_custom_call" | custom-call | tf_op jit(solution)/shard_map/gather_texts/pallas_call | solution.py:190
  32.1 4.8 %all-to-all-start.1 = ((bf16[4,64,1152]{2,1,0:T(8,128)(2,1)}), bf16[4,64,1152]{2,1,0:T(8,128)(2,1)S(1)}, u32[]{:S(2)}, u32[]{:S(2)}) async-start(bf16[4,64,1152]{2,1,0:T(8,128)(2,1)} %gather_texts.3), calls=%async_computation.1 | async-start | bytes 1179648 | tf_op jit(solution)/shard_map/gather_texts/all_to_all | solution.py:29
  38.8 0.1 broadcast_add_fusion.1.columns
  38.9 0.0 copy-done
  38.9 0.0 copy-done.1
  38.9 1.1 %swap_images.1 = (bf16[272,1152]{1,0:T(8,128)(2,1)}, bf16[272,1152]{1,0:T(8,128)(2,1)}) custom-call(bf16[512,1152]{1,0:T(8,128)(2,1)S(1)} %copy-done, s32[1,512]{1,0:T(1,128)S(1)} %bitcast.2, bf16[64,2,576]{2,1,0:T(2,128)(2,1)S(1)} %all_to_all.20.halves.after), custom_call_target="tpu_custom_call" | custom-call | bytes 2359296 | tf_op jit(solution)/shard_map/swap_images/pallas_call | solution.py:201
  40.0 1.9 %collective-permute-start.2 = (bf16[272,1152]{1,0:T(8,128)(2,1)}, bf16[272,1152]{1,0:T(8,128)(2,1)S(1)}, u32[]{:S(2)}, u32[]{:S(2)}) collective-permute-start(bf16[272,1152]{1,0:T(8,128)(2,1)} %get-tuple-element.15), channel_id=1, source_target_pairs={{0,16},{16,0},{1,17},{17,1},{2,18},{18,2},{3,19},{19,3},{4,20},{20... | collective-permute-start | bytes 1880072 | tf_op jit(solution)/shard_map/swap_images/ppermute | solution.py:25
  41.9 2.4 %collective-permute-start.3 = (bf16[272,1152]{1,0:T(8,128)(2,1)}, bf16[272,1152]{1,0:T(8,128)(2,1)}, u32[]{:S(2)}, u32[]{:S(2)}) collective-permute-start(bf16[272,1152]{1,0:T(8,128)(2,1)} %get-tuple-element.16), channel_id=1, source_target_pairs={{0,16},{16,0},{1,17},{17,1},{2,18},{18,2},{3,19},{19,3},{4,20},{20... | collective-permute-start | bytes 1880072 | tf_op jit(solution)/shard_map/swap_images/ppermute | solution.py:25
  44.3 0.0 all-to-all-done.1.texts
  44.3 1.1 %coefficients.2 = (bf16[256,512]{1,0:T(8,128)(2,1)S(1)}, f32[8,128]{1,0:T(8,128)S(1)}, bf16[2,64,1152]{2,1,0:T(8,128)(2,1)}, bf16[2,64,1152]{2,1,0:T(8,128)(2,1)}) custom-call(f32[1]{0:T(128)S(6)} %copy.8.log_scale, f32[1]{0:T(128)S(6)} %copy.9.bias, f32[1]{0:T(128)S(6)} %copy.10.loss_scale, s32[256,1]{1,0:T(8,128)S(1)} %broadcast_add_fusion.1.columns, ...), custom_call_target="tpu_custom_call" | custom-call | flops 17179869184 | bytes 2359296 | tf_op jit(solution)/shard_map/coefficients/pallas_call | solution.py:217
  45.4 0.0 collective-permute-done.2.refs_0_
  45.4 0.9 %collective-permute-done.3.refs_1_ = bf16[272,1152]{1,0:T(8,128)(2,1)} collective-permute-done((bf16[272,1152]{1,0:T(8,128)(2,1)}, bf16[272,1152]{1,0:T(8,128)(2,1)}, u32[]{:S(2)}, u32[]{:S(2)}) %collective-permute-start.3) | collective-permute-done | bytes 626720 | tf_op jit(solution)/shard_map/swap_images/ppermute | solution.py:25
  46.3 3.3 %coefficients.3 = bf16[256,1152]{1,0:T(8,128)(2,1)} custom-call(f32[8,128]{1,0:T(8,128)S(1)} %get-tuple-element.10.rows, s32[256,1]{1,0:T(8,128)S(1)} %broadcast_add_fusion.1.columns, bf16[4,64,1152]{2,1,0:T(8,128)(2,1)S(1)} %all-to-all-done.1.texts, bf16[256,512]{1,0:T(8,128)(2,1)S(1)} %get-tuple-element.11.coef, bf16[512,1152]{1,0:T(8,128)(2,1)S(1)} %copy-done, ...), custom_call_target="tpu_custom_call" | custom-call | flops 905969664 | bytes 2359296 | tf_op jit(solution)/shard_map/coefficients/pallas_call | solution.py:238
  49.6 0.0 copy-start.3
  49.6 4.9 %all-to-all-start.2 = ((bf16[4,64,1152]{2,1,0:T(8,128)(2,1)}), bf16[4,64,1152]{2,1,0:T(8,128)(2,1)S(1)}, u32[]{:S(2)}, u32[]{:S(2)}) async-start(bf16[4,64,1152]{2,1,0:T(8,128)(2,1)} %bitcast.1), calls=%async_computation.2 | async-start | bytes 1179648 | tf_op jit(solution)/shard_map/text_grad/all_to_all | solution.py:29
  54.5 1.9 %collective-permute-start = (bf16[2,64,1152]{2,1,0:T(8,128)(2,1)}, bf16[2,64,1152]{2,1,0:T(8,128)(2,1)S(1)}, u32[]{:S(2)}, u32[]{:S(2)}) collective-permute-start(bf16[2,64,1152]{2,1,0:T(8,128)(2,1)} %get-tuple-element.12), channel_id=1, source_target_pairs={{0,16},{16,0},{1,17},{17,1},{2,18},{18,2},{3,19},{19,3},{4,20},{20... | collective-permute-start | bytes 884744 | tf_op jit(solution)/shard_map/image_grad/ppermute | solution.py:25
  56.5 0.0 copy-done.3
  56.5 2.4 %collective-permute-start.1 = (bf16[2,64,1152]{2,1,0:T(8,128)(2,1)S(1)}, bf16[2,64,1152]{2,1,0:T(8,128)(2,1)S(1)}, u32[]{:S(2)}, u32[]{:S(2)}) collective-permute-start(bf16[2,64,1152]{2,1,0:T(8,128)(2,1)S(1)} %copy-done.3), channel_id=1, source_target_pairs={{0,16},{16,0},{1,17},{17,1},{2,18},{18,2},{3,19},{19,3},{4,20},{20... | collective-permute-start | bytes 884744 | tf_op jit(solution)/shard_map/image_grad/ppermute | solution.py:25
  58.9 0.1 broadcast_add_fusion.columns
  58.9 0.0 collective-permute-done.refs_0_
  59.0 1.1 %collective-permute-done.1.refs_1_ = bf16[2,64,1152]{2,1,0:T(8,128)(2,1)S(1)} collective-permute-done((bf16[2,64,1152]{2,1,0:T(8,128)(2,1)S(1)}, bf16[2,64,1152]{2,1,0:T(8,128)(2,1)S(1)}, u32[]{:S(2)}, u32[]{:S(2)}) %collective-permute-start.1) | collective-permute-done | bytes 294944 | tf_op jit(solution)/shard_map/image_grad/ppermute | solution.py:25
  60.1 2.3 %image_grad.1 = (bf16[512,1152]{1,0:T(8,128)(2,1)}, f32[8,128]{1,0:T(8,128)S(1)}) custom-call(f32[8,128]{1,0:T(8,128)S(1)} %get-tuple-element.10.rows, s32[256,1]{1,0:T(8,128)S(1)} %broadcast_add_fusion.columns, s32[1,512]{1,0:T(1,128)S(1)} %bitcast.4, bf16[256,512]{1,0:T(8,128)(2,1)S(1)} %get-tuple-element.11.coef, ...), custom_call_target="tpu_custom_call" | custom-call | tf_op jit(solution)/shard_map/image_grad/pallas_call | solution.py:253
  62.4 0.8 all-to-all-done.2.blocks
  63.2 0.2 text_grad.2
  63.4 17.1 %all_to_all.21.parts = bf16[64,2,576]{2,1,0:T(2,128)(2,1)S(1)} all-to-all(bf16[64,2,576]{2,1,0:T(2,128)(2,1)S(1)} %text_grad.2), channel_id=1, replica_groups=mesh['far'=16,'core'=2,'x'=4,'zl'=4] {'far','zl'}, dimensions={0} | all-to-all | bytes 294912 | tf_op jit(solution)/shard_map/text_grad/all_to_all | solution.py:29
  80.4 0.8 %text_grad.3 = bf16[1,1152]{1,0:T(2,128)(2,1)} custom-call(bf16[64,2,576]{2,1,0:T(2,128)(2,1)S(1)} %all_to_all.21.parts), custom_call_target="tpu_custom_call" | custom-call | tf_op jit(solution)/shard_map/text_grad/pallas_call | solution.py:278
Async XLA Ops:
  0.6 0.7 copy-start.2
  1.4 37.5 %copy-start = (bf16[512,1152]{1,0:T(8,128)(2,1)S(1)}, bf16[512,1152]{1,0:T(8,128)(2,1)}, u32[]{:S(2)}) copy-start(bf16[512,1152]{1,0:T(8,128)(2,1)} %images.5) | copy-start | bytes 3538948
  1.4 37.5 %copy-start.1 = (s32[512]{0:T(512)S(1)}, s32[512]{0:T(512)}, u32[]{:S(2)}) copy-start(s32[512]{0:T(512)} %param.8) | copy-start | bytes 6148
  32.1 12.2 %all-to-all-start.1 = ((bf16[4,64,1152]{2,1,0:T(8,128)(2,1)}), bf16[4,64,1152]{2,1,0:T(8,128)(2,1)S(1)}, u32[]{:S(2)}, u32[]{:S(2)}) async-start(bf16[4,64,1152]{2,1,0:T(8,128)(2,1)} %gather_texts.3), calls=%async_computation.1 | async-start | bytes 1179648 | tf_op jit(solution)/shard_map/gather_texts/all_to_all | solution.py:29
  40.0 5.4 %collective-permute-start.2 = (bf16[272,1152]{1,0:T(8,128)(2,1)}, bf16[272,1152]{1,0:T(8,128)(2,1)S(1)}, u32[]{:S(2)}, u32[]{:S(2)}) collective-permute-start(bf16[272,1152]{1,0:T(8,128)(2,1)} %get-tuple-element.15), channel_id=1, source_target_pairs={{0,16},{16,0},{1,17},{17,1},{2,18},{18,2},{3,19},{19,3},{4,20},{20... | collective-permute-start | bytes 1880072 | tf_op jit(solution)/shard_map/swap_images/ppermute | solution.py:25
  41.9 4.4 %collective-permute-start.3 = (bf16[272,1152]{1,0:T(8,128)(2,1)}, bf16[272,1152]{1,0:T(8,128)(2,1)}, u32[]{:S(2)}, u32[]{:S(2)}) collective-permute-start(bf16[272,1152]{1,0:T(8,128)(2,1)} %get-tuple-element.16), channel_id=1, source_target_pairs={{0,16},{16,0},{1,17},{17,1},{2,18},{18,2},{3,19},{19,3},{4,20},{20... | collective-permute-start | bytes 1880072 | tf_op jit(solution)/shard_map/swap_images/ppermute | solution.py:25
  49.6 6.9 %copy-start.3 = (bf16[2,64,1152]{2,1,0:T(8,128)(2,1)S(1)}, bf16[2,64,1152]{2,1,0:T(8,128)(2,1)}, u32[]{:S(2)}) copy-start(bf16[2,64,1152]{2,1,0:T(8,128)(2,1)} %get-tuple-element.13) | copy-start | bytes 884740
  49.6 13.6 %all-to-all-start.2 = ((bf16[4,64,1152]{2,1,0:T(8,128)(2,1)}), bf16[4,64,1152]{2,1,0:T(8,128)(2,1)S(1)}, u32[]{:S(2)}, u32[]{:S(2)}) async-start(bf16[4,64,1152]{2,1,0:T(8,128)(2,1)} %bitcast.1), calls=%async_computation.2 | async-start | bytes 1179648 | tf_op jit(solution)/shard_map/text_grad/all_to_all | solution.py:29
  54.5 4.4 %collective-permute-start = (bf16[2,64,1152]{2,1,0:T(8,128)(2,1)}, bf16[2,64,1152]{2,1,0:T(8,128)(2,1)S(1)}, u32[]{:S(2)}, u32[]{:S(2)}) collective-permute-start(bf16[2,64,1152]{2,1,0:T(8,128)(2,1)} %get-tuple-element.12), channel_id=1, source_target_pairs={{0,16},{16,0},{1,17},{17,1},{2,18},{18,2},{3,19},{19,3},{4,20},{20... | collective-permute-start | bytes 884744 | tf_op jit(solution)/shard_map/image_grad/ppermute | solution.py:25
  56.5 3.6 %collective-permute-start.1 = (bf16[2,64,1152]{2,1,0:T(8,128)(2,1)S(1)}, bf16[2,64,1152]{2,1,0:T(8,128)(2,1)S(1)}, u32[]{:S(2)}, u32[]{:S(2)}) collective-permute-start(bf16[2,64,1152]{2,1,0:T(8,128)(2,1)S(1)} %copy-done.3), channel_id=1, source_target_pairs={{0,16},{16,0},{1,17},{17,1},{2,18},{18,2},{3,19},{19,3},{4,20},{20... | collective-permute-start | bytes 884744 | tf_op jit(solution)/shard_map/image_grad/ppermute | solution.py:25
